TPU v7x, 32 devices: a whole 2x2x4 slice. The times are simulated.
32 devices in a mesh: group: 2 (over y), row: 8 (over z, x), epoch: 2 (over core).
Axes of the slice: x: 2, y: 2, z: 4, core: 2. Of those that a mesh axis runs over, the one named last changes fastest.
Arguments:
- images: bfloat16 [8, 2048, 2048], P(('group', 'epoch'), 'row'), parts along dimension 0, may hold values from -6 to 6
- rate_vectors: int32 [2, 2], replicated, may hold values from -192 to 192
- epoch_times: int32 [4], replicated, may hold values from 0 to 127
Outputs:
- rate_images: float32 [4, 2048, 2048], P(('group', 'epoch'), 'row'), parts along dimension 0
There are 2 independent parts, one for each index of `group`. A program takes and returns all parts, laid end to end along the dimension named above; an argument that names none is the same for every part. Nothing has to cross between parts.
All inputs are finite; a program needn't handle non-finite values.
Results may differ from a plain program's by a relative error of at most 0.011.
Values may be sent and summed in bfloat16 or wider, within the bound.
A program may use at most 128 MiB of HBM per device.

v0:
```python
import math

import jax
import jax.numpy as jnp
from jax import lax
from jax.sharding import PartitionSpec as P

SUBPIX = 16


def dft_tables(length):
    positions = jnp.arange(length, dtype=jnp.int32)
    turn_count = positions[:, None] * positions[None, :] % length
    angles = turn_count.astype(jnp.float32) * (2.0 * math.pi / length)
    factor = 1.0 / math.sqrt(length)
    return (
        (jnp.cos(angles) * factor).astype(jnp.bfloat16),
        (jnp.sin(angles) * factor).astype(jnp.bfloat16),
    )


def ramp_sums(spectrum, freq_rows, freq_cols, rate_vectors, time_steps, length):
    period = SUBPIX * length
    real_part = spectrum[:, 0].astype(jnp.float32)
    imag_part = spectrum[:, 1].astype(jnp.float32)

    def one_rate(rate_row):
        shift_y = rate_row[0] * time_steps % period
        shift_x = rate_row[1] * time_steps % period
        row_turns = shift_y[:, None] * freq_rows[None, :] % period
        col_turns = freq_cols[:, None] * shift_x[None, :] % period
        row_angles = row_turns.astype(jnp.float32) * (2.0 * math.pi / period)
        col_angles = col_turns.astype(jnp.float32) * (2.0 * math.pi / period)
        row_cos = jnp.cos(row_angles)[None]
        row_sin = jnp.sin(row_angles)[None]
        col_cos = jnp.cos(col_angles)[:, :, None]
        col_sin = jnp.sin(col_angles)[:, :, None]
        ramp_re = col_cos * row_cos - col_sin * row_sin
        ramp_im = col_sin * row_cos + col_cos * row_sin
        summed_re = jnp.sum(real_part * ramp_re - imag_part * ramp_im, axis=1)
        summed_im = jnp.sum(real_part * ramp_im + imag_part * ramp_re, axis=1)
        return jnp.stack([summed_re, summed_im], axis=1)

    return lax.map(one_rate, rate_vectors)


def local(images, rate_vectors, epoch_times):
    loc_epochs, loc_rows, length = images.shape
    row_count = lax.axis_size("row")
    epoch_count = lax.axis_size("epoch")
    row_pos = lax.axis_index("row")
    epoch_pos = lax.axis_index("epoch")
    loc_cols = length // row_count
    cosine, sine = dft_tables(length)
    stacked = jnp.stack([cosine, sine])
    stack_scale = 1.0 / math.sqrt(epoch_times.shape[0])
    sign_wide = jnp.array([1.0, -1.0], jnp.float32)[:, None]
    sign_narrow = jnp.array([1.0, -1.0], jnp.bfloat16)[:, None]
    row_terms = jnp.einsum("tcv,elc->vetl", stacked, images, preferred_element_type=jnp.float32)
    row_spectrum = (row_terms * sign_wide).astype(jnp.bfloat16)
    narrow = loc_cols // epoch_count
    gathered = lax.all_to_all(
        lax.all_to_all(row_spectrum, "row", split_axis=0, concat_axis=3, tiled=True),
        "epoch",
        split_axis=0,
        concat_axis=1,
        tiled=True,
    )
    products = jnp.einsum("vetr,wru->wvteu", gathered, stacked, preferred_element_type=jnp.float32)
    real_part = products[0, :, 0] + products[1, :, 1]
    imag_part = products[0, :, 1] - products[1, :, 0]
    spectra = jnp.stack([real_part, imag_part], axis=1).astype(jnp.bfloat16)
    freq_cols = row_pos * loc_cols + epoch_pos * narrow + jnp.arange(narrow, dtype=jnp.int32)
    freq_rows = jnp.arange(length, dtype=jnp.int32)
    rate_sums = ramp_sums(spectra, freq_rows, freq_cols, rate_vectors, epoch_times, length)
    rate_spectrum = (rate_sums * stack_scale).astype(jnp.bfloat16)
    products = jnp.einsum(
        "kvtu,wur->wkrtv", rate_spectrum, stacked, preferred_element_type=jnp.float32
    )
    real_part = products[0, :, :, 0] - products[1, :, :, 1]
    imag_part = products[0, :, :, 1] + products[1, :, :, 0]
    columns_back = jnp.stack([real_part, imag_part], axis=2).astype(jnp.bfloat16)
    returned = lax.all_to_all(
        lax.all_to_all(columns_back, "row", split_axis=1, concat_axis=3, tiled=True),
        "epoch",
        split_axis=0,
        concat_axis=3,
        tiled=True,
    )
    signed = returned * sign_narrow
    reshaped = signed.reshape(signed.shape[0], signed.shape[1], 2, epoch_count, row_count, narrow)
    inverse_table = stacked.reshape(2, row_count, epoch_count, narrow, length)
    result_rows = jnp.einsum(
        "krtjiw,tijwc->krc", reshaped, inverse_table, preferred_element_type=jnp.float32
    )
    return result_rows


def solution(mesh):
    in_specs = (P(("group", "epoch"), "row", None), P(), P())
    out_specs = P(("group", "epoch"), "row", None)
    return jax.shard_map(local, mesh=mesh, in_specs=in_specs, out_specs=out_specs, check_vma=False)
```

profile of v0, /device:TPU:0, one launch (start us, length us, event | category | flops | bytes accessed | tf_op | source)
XLA Modules:
  0.0 449.5 jit_solution(12149800663286219467)
XLA Ops:
  0.0 68.6 %multiply_convert_fusion.2 = (bf16[1,2048,2048]{1,2,0:T(8,128)(2,1)S(1)}, bf16[1,2048,2048]{1,2,0:T(8,128)(2,1)}) fusion(), kind=kLoop, calls=%fused_computation.64 | loop fusion | flops 75497472 | bytes 16777216 | tf_op jit(solution)/shard_map/convert_element_type | solution.py:18
  68.6 14.7 %fusion.49 = bf16[2048,2,2,256]{3,0,1,2:T(8,128)(2,1)S(1)} fusion(f32[2]{0:T(128)S(1)} %copy-done.7, bf16[1,2048,2048]{1,2,0:T(8,128)(2,1)S(1)} %get-tuple-element.189, bf16[1,2048,2048]{1,2,0:T(8,128)(2,1)} %get-tuple-element.190, bf16[2,256,2048]{2,1,0:T(8,128)(2,1)S(1)} %copy-done), kind=kOutput, calls=%fused_computation.78 | convolution fusion | flops 8627683328 | bytes 23068680 | tf_op jit(solution)/shard_map/tcv,elc->vetl/dot_general | solution.py:59
  83.3 19.1 %copy.52 = bf16[2048,2,2,256]{3,1,2,0:T(2,128)(2,1)} copy(bf16[2048,2,2,256]{3,0,1,2:T(8,128)(2,1)S(1)} %fusion.49) | data formatting | bytes 8388608 | tf_op jit(solution)/shard_map/convert_element_type | solution.py:60
  102.4 7.3 %all-to-all-start = ((bf16[2048,2,2,256]{3,1,2,0:T(2,128)(2,1)}), bf16[2048,2,2,256]{3,1,2,0:T(2,128)(2,1)}, u32[]{:S(2)}, u32[]{:S(2)}) async-start(bf16[2048,2,2,256]{3,1,2,0:T(2,128)(2,1)} %copy.52), calls=%async_computation | async-start | bytes 8388608 | tf_op jit(solution)/shard_map/all_to_all | solution.py:63
  109.7 93.3 %all-to-all-done = bf16[2048,2,2,256]{3,1,2,0:T(2,128)(2,1)} async-done(((bf16[2048,2,2,256]{3,1,2,0:T(2,128)(2,1)}), bf16[2048,2,2,256]{3,1,2,0:T(2,128)(2,1)}, u32[]{:S(2)}, u32[]{:S(2)}) %all-to-all-start) | async-done | bytes 4194336 | tf_op jit(solution)/shard_map/all_to_all | solution.py:63
  203.0 4.7 %copy.53 = bf16[2048,2,2,256]{3,0,2,1:T(8,128)(2,1)} copy(bf16[2048,2,2,256]{3,1,2,0:T(2,128)(2,1)} %all-to-all-done) | data formatting | bytes 8388608 | tf_op jit(solution)/shard_map/all_to_all | solution.py:63
  207.7 6.2 %copy.54 = bf16[256,2,2,8,256]{0,4,3,2,1:T(8,128)(2,1)} copy(bf16[256,2,2,8,256]{4,0,3,2,1:T(8,128)(2,1)} %bitcast.97) | data formatting | bytes 8388608 | tf_op jit(solution)/shard_map/all_to_all | solution.py:63
  213.9 11.2 %copy.55 = bf16[256,2,2,2048]{3,2,1,0:T(2,128)(2,1)} copy(bf16[256,2,2,2048]{0,3,2,1:T(8,128)(2,1)} %bitcast.98) | data formatting | bytes 8388608 | tf_op jit(solution)/shard_map/all_to_all | solution.py:63
  225.1 8.9 %all_to_all.72 = bf16[256,2,2,2048]{3,2,1,0:T(2,128)(2,1)S(1)} all-to-all(bf16[256,2,2,2048]{3,2,1,0:T(2,128)(2,1)} %copy.55), channel_id=1, replica_groups=mesh['group'=2,'row'=8,'epoch'=2] {'epoch'}, dimensions={0} | all-to-all | bytes 8388608 | tf_op jit(solution)/shard_map/all_to_all | solution.py:62
  240.4 22.7 %fusion.39 = f32[2,128,2,4,2048]{1,4,2,3,0:T(8,128)} fusion(bf16[128,4,2,2048,1]{3,0,2,1,4:T(8,128)(2,1)} %bitcast.107, bf16[1,2048,2048]{1,2,0:T(8,128)(2,1)S(1)} %bitcast.101, bf16[1,2048,2048]{1,2,0:T(8,128)(2,1)S(1)} %bitcast.103), kind=kOutput, calls=%fused_computation.71 | convolution fusion | flops 17213423616 | bytes 37748736 | tf_op jit(solution)/shard_map/vetr,wru->wvteu/dot_general | solution.py:69
  263.2 9.9 %fusion.58 = (f32[128,4,2048]{0,2,1:T(8,128)}, f32[128,4,2048]{0,2,1:T(8,128)}) fusion(f32[2,128,2,4,2048]{1,4,2,3,0:T(8,128)} %fusion.39), kind=kLoop, calls=%fused_computation.83 | loop fusion | flops 6291456 | bytes 25165824 | tf_op jit(solution)/shard_map/convert_element_type | solution.py:25
  273.1 5.5 %copy.58 = f32[128,4,2048]{2,1,0:T(4,128)} copy(f32[128,4,2048]{0,2,1:T(8,128)} %get-tuple-element.186) | data formatting | bytes 8388608
  278.6 5.5 %copy.59 = f32[128,4,2048]{2,1,0:T(4,128)} copy(f32[128,4,2048]{0,2,1:T(8,128)} %get-tuple-element.185) | data formatting | bytes 8388608
  284.1 39.6 %while.13 = (s32[]{:T(128)}, f32[2,128,2,2048]{3,2,1,0:T(2,128)}, s32[2,2]{1,0:T(2,128)S(1)}, s32[4]{0:T(128)S(1)}, f32[128,4,2048]{2,1,0:T(4,128)}, /*index=5*/f32[128,4,2048]{2,1,0:T(4,128)}, s32[]{:T(128)}, s32[]{:T(128)}) while((s32[]{:T(128)}, f32[2,128,2,2048]{3,2,1,0:T(2,128)}, s32[2,2]{1,0:T(2,128)S(1)}, s32[4]{0:T(128)S(1)}, ...), condition=%wide.region_3.4_spmd.clone, body=%wide.region_0.3_spmd.clone.sunk | while | flops 14802146 | bytes 19023572 | solution.py:44
  286.8 12.4 %subtract_reduce_fusion.2 = (f32[128,2048]{1,0:T(8,128)S(1)}, f32[128,2048]{1,0:T(8,128)S(1)}) fusion(f32[128,4,2048]{2,1,0:T(4,128)} %get-tuple-element.275, f32[128,4,2048]{2,1,0:T(4,128)} %get-tuple-element.274, f32[4,2048]{1,0:T(4,128)S(1)} %get-tuple-element.247, f32[128,4]{1,0:T(8,128)S(1)} %copy.83, f32[4,2048]{1,0:T(4,128)S(1)} %get-tuple-element.250, ...), kind=kLoop, calls=%fused_computation.3.clone.1 | loop fusion | flops 14155776 | bytes 10555392 | tf_op jit(solution)/shard_map/while/body/eval_jaxpr/reduce_sum | solution.py:40
  306.4 12.4 %subtract_reduce_fusion.2 = (f32[128,2048]{1,0:T(8,128)S(1)}, f32[128,2048]{1,0:T(8,128)S(1)}) fusion(f32[128,4,2048]{2,1,0:T(4,128)} %get-tuple-element.275, f32[128,4,2048]{2,1,0:T(4,128)} %get-tuple-element.274, f32[4,2048]{1,0:T(4,128)S(1)} %get-tuple-element.247, f32[128,4]{1,0:T(8,128)S(1)} %copy.83, f32[4,2048]{1,0:T(4,128)S(1)} %get-tuple-element.250, ...), kind=kLoop, calls=%fused_computation.3.clone.1 | loop fusion | flops 14155776 | bytes 10555392 | tf_op jit(solution)/shard_map/while/body/eval_jaxpr/reduce_sum | solution.py:40
  320.3 3.3 fusion.81
  323.6 4.3 multiply_convert_fusion.5
  328.0 12.9 %fusion.44 = f32[2,2,2048,2,128]{4,2,3,1,0:T(8,128)S(1)} fusion(bf16[1,2048,2048]{1,2,0:T(8,128)(2,1)} %copy-done.2, bf16[1,2048,2048]{1,2,0:T(8,128)(2,1)} %get-tuple-element.190, bf16[2,128,2,2048]{3,2,1,0:T(2,128)(2,1)S(1)} %multiply_convert_fusion.5), kind=kOutput, calls=%fused_computation.72 | convolution fusion | flops 8623489024 | bytes 27262976 | tf_op jit(solution)/shard_map/kvtu,wur->wkrtv/dot_general | solution.py:77
  341.5 14.0 %copy.63 = bf16[2,2048,2,128]{3,0,2,1:T(2,128)(2,1)} copy(bf16[2,2048,2,128]{3,1,0,2:T(8,128)(2,1)S(1)} %pad_maximum_fusion.4) | data formatting | bytes 4194304 | tf_op jit(solution)/shard_map/stack | solution.py:82
  355.5 3.6 all-to-all-start.2
  359.1 71.3 %multiply_convert_fusion.1 = (bf16[1,8,2,128,2048]{4,3,0,2,1:T(8,128)(2,1)}, bf16[1,8,2,128,2048]{4,3,0,2,1:T(8,128)(2,1)}) fusion(s32[8,2,128]{2,1,0:T(2,128)S(1)} %multiply_add_fusion.1), kind=kLoop, calls=%fused_computation.61 | loop fusion | flops 75497472 | bytes 16785408 | tf_op jit(solution)/shard_map/convert_element_type | solution.py:17
  434.8 5.8 %all_to_all.73 = bf16[2,256,2,1024]{1,3,2,0:T(8,128)(2,1)S(1)} all-to-all(bf16[2,256,2,1024]{1,3,2,0:T(8,128)(2,1)S(1)} %bitcast.105), channel_id=1, replica_groups=mesh['group'=2,'row'=8,'epoch'=2] {'epoch'}, dimensions={0} | all-to-all | bytes 4194304 | tf_op jit(solution)/shard_map/all_to_all | solution.py:83
  440.8 8.3 %fusion.52 = f32[1,256,2048]{2,1,0:T(8,128)} fusion(bf16[1,8,2,128,2048]{4,3,0,2,1:T(8,128)(2,1)} %get-tuple-element.188, bf16[1,8,2,128,2048]{4,3,0,2,1:T(8,128)(2,1)S(1)} %copy-done.3, bf16[256,2,2,8,128]{0,4,3,2,1:T(8,128)(2,1)S(1)} %bitcast.108, bf16[2]{0:T(256)(128)(2,1)S(1)} %copy-done.6), kind=kOutput, calls=%fused_computation.79 | convolution fusion | flops 4304404480 | bytes 20971524 | tf_op jit(solution)/shard_map/krtjiw,tijwc->krc/dot_general | solution.py:93
  (58 shorter events, 22.7 us)
Async XLA Ops:
  0.0 68.6 %copy-start = (bf16[2,256,2048]{2,1,0:T(8,128)(2,1)S(1)}, bf16[2,256,2048]{2,1,0:T(8,128)(2,1)}, u32[]{:S(2)}) copy-start(bf16[2,256,2048]{2,1,0:T(8,128)(2,1)} %param.7) | copy-start | bytes 6291460
  0.0 68.6 %copy-start.7 = (f32[2]{0:T(128)S(1)}, f32[2]{0:T(128)}, u32[]{:S(2)}) copy-start(f32[2]{0:T(128)} %constant.114.clone) | copy-start | bytes 28
  68.6 14.7 %copy-start.2 = (bf16[1,2048,2048]{1,2,0:T(8,128)(2,1)}, bf16[1,2048,2048]{1,2,0:T(8,128)(2,1)S(1)}, u32[]{:S(2)}) copy-start(bf16[1,2048,2048]{1,2,0:T(8,128)(2,1)S(1)} %get-tuple-element.189) | copy-start | bytes 25165828
  102.4 100.5 %all-to-all-start = ((bf16[2048,2,2,256]{3,1,2,0:T(2,128)(2,1)}), bf16[2048,2,2,256]{3,1,2,0:T(2,128)(2,1)}, u32[]{:S(2)}, u32[]{:S(2)}) async-start(bf16[2048,2,2,256]{3,1,2,0:T(2,128)(2,1)} %copy.52), calls=%async_computation | async-start | bytes 8388608 | tf_op jit(solution)/shard_map/all_to_all | solution.py:63
  225.1 13.7 %slice-start.2 = ((s8[8388608]{0:T(1024)(128)(4,1)}), s8[4194304]{0:T(1024)(128)(4,1)S(1)}, s32[]{:S(2)}) async-start(s8[8388608]{0:T(1024)(128)(4,1)} %bitcast.102), calls=%async_computation.6 | async-start | bytes 8388608
  234.0 4.8 %slice-start = ((s8[8388608]{0:T(1024)(128)(4,1)}), s8[4194304]{0:T(1024)(128)(4,1)S(1)}, s32[]{:S(2)}) async-start(s8[8388608]{0:T(1024)(128)(4,1)} %bitcast.100), calls=%async_computation.4 | async-start | bytes 8388608
  234.0 4.8 %slice-start.3 = ((s8[8388608]{0:T(1024)(128)(4,1)}), s8[4194304]{0:T(1024)(128)(4,1)S(1)}, s32[]{:S(2)}) async-start(s8[8388608]{0:T(1024)(128)(4,1)} %bitcast.102), calls=%async_computation.7 | async-start | bytes 8388608
  236.3 4.1 slice-start.1
  278.5 5.5 %copy-start.4 = (s32[4]{0:T(128)S(1)}, s32[4]{0:T(128)}, u32[]{:S(2)}) copy-start(s32[4]{0:T(128)} %param.9) | copy-start | bytes 52
  278.5 5.5 %copy-start.5 = (s32[2,2]{1,0:T(2,128)S(1)}, s32[2,2]{1,0:T(2,128)}, u32[]{:S(2)}) copy-start(s32[2,2]{1,0:T(2,128)} %param.8) | copy-start | bytes 52
  355.5 74.9 %all-to-all-start.2 = ((bf16[2,2048,2,128]{3,0,2,1:T(2,128)(2,1)}), bf16[2,2048,2,128]{3,0,2,1:T(2,128)(2,1)S(1)}, u32[]{:S(2)}, u32[]{:S(2)}) async-start(bf16[2,2048,2,128]{3,0,2,1:T(2,128)(2,1)} %copy.63), calls=%async_computation.2 | async-start | bytes 4194304 | tf_op jit(solution)/shard_map/all_to_all | solution.py:84
  434.8 6.0 %copy-start.3 = (bf16[1,8,2,128,2048]{4,3,0,2,1:T(8,128)(2,1)S(1)}, bf16[1,8,2,128,2048]{4,3,0,2,1:T(8,128)(2,1)}, u32[]{:S(2)}) copy-start(bf16[1,8,2,128,2048]{4,3,0,2,1:T(8,128)(2,1)} %get-tuple-element.187) | copy-start | bytes 25165828
  434.8 6.0 %copy-start.6 = (bf16[2]{0:T(256)(128)(2,1)S(1)}, bf16[2]{0:T(256)(128)(2,1)}, u32[]{:S(2)}) copy-start(bf16[2]{0:T(256)(128)(2,1)} %constant.115.clone) | copy-start | bytes 16
  440.8 8.3 %copy-start.1 = (bf16[2,256,2048]{2,1,0:T(8,128)(2,1)S(1)}, bf16[2,256,2048]{2,1,0:T(8,128)(2,1)}, u32[]{:S(2)}) copy-start(bf16[2,256,2048]{2,1,0:T(8,128)(2,1)} %param.7) | copy-start | bytes 6291460
where the time goes:
time: 458 us; the launch traced here: 450 us
  other arithmetic  189 us (41%)
  waiting for transfers between devices  93.3 us (20%)
  local copies, waits for them, and re-layouts  81.8 us (18%)
  matrix products  58.5 us (13%)
  blocking collectives  14.7 us (3%)
  starting transfers between devices  10.9 us (2%)
    all_to_all x1, waiting for transfers between devices, local(): lax.all_to_all(row_spectrum, 'row', split_axis=0, concat_axis=3, tiled=True)  93.3 us
    convert_element_type x1, other arithmetic, dft_tables(): (jnp.cos(angles) * factor).astype(jnp.bfloat16)  71.3 us
    convert_element_type x1, other arithmetic, dft_tables(): (jnp.sin(angles) * factor).astype(jnp.bfloat16)  68.6 us
    reduce_sum x2, other arithmetic, one_rate(): summed_re = jnp.sum(real_part * ramp_re - imag_part * ramp_im, axis=1)  24.9 us
    dot_general x1, matrix products, local(): jnp.einsum('vetr,wru->wvteu', gathered, stacked, preferred_element_type=j...  22.7 us
    all_to_all x3, local copies, waits for them, and re-layouts, local(): lax.all_to_all(row_spectrum, 'row', split_axis=0, concat_axis=3, tiled=True)  22.2 us
    convert_element_type x1, local copies, waits for them, and re-layouts, local(): row_spectrum = (row_terms * sign_wide).astype(jnp.bfloat16)  19.1 us
    dot_general x1, matrix products, local(): jnp.einsum('tcv,elc->vetl', stacked, images, preferred_element_type=jnp.f...  14.7 us
  transfers between devices with their start and end apart: 2, of which 1 were waited for; matrix products, arithmetic and copies ran while one was open for 16% of the time, Pallas kernels for 0%

commit v1 on v0

v1 whole, which is shorter than its diff:
```python
import functools
import math

import jax
import jax.numpy as jnp
import ml_dtypes
import numpy as np
from jax import lax
from jax.sharding import PartitionSpec as P

SUBPIX = 16


@functools.lru_cache(maxsize=None)
def real_table(length):
    half = length // 2
    positions = np.arange(length, dtype=np.int64)
    turns = (positions[:half, None] * positions[None, :]) % length
    angles = turns * (2.0 * math.pi / length)
    factor = 1.0 / math.sqrt(length)
    nyquist = 1.0 - 2.0 * (positions % 2)
    table = np.concatenate([np.cos(angles), nyquist[None], np.sin(angles)[1:]]) * factor
    return table.astype(np.float32).astype(ml_dtypes.bfloat16)


def lane_order(length, devices):
    half = length // 2
    slots = np.arange(half).reshape(devices, 1, half // devices)
    return np.concatenate([slots, slots + half], axis=1).reshape(-1)


def turn_cos_sin(turns, period):
    angles = (turns % period).astype(jnp.float32) * (2.0 * math.pi / period)
    return jnp.cos(angles), jnp.sin(angles)


def coefficients(rate_vectors, epoch_times, first_slot, slots, length):
    period = SUBPIX * length
    half = length // 2
    scale = 1.0 / math.sqrt(epoch_times.shape[0])
    shift_y = rate_vectors[:, 0:1] * epoch_times[None, :] % period
    shift_x = rate_vectors[:, 1:2] * epoch_times[None, :] % period
    freq = jnp.arange(half, dtype=jnp.int32)
    row_cos, row_sin = turn_cos_sin((freq - half) * shift_y[:, :, None], period)
    row_cos = jnp.where(freq == 0, 1.0, 2.0 * row_cos)
    row_sin = jnp.where(freq == 0, 0.0, 2.0 * row_sin)
    slot = first_slot + jnp.arange(slots, dtype=jnp.int32)
    col_cos, col_sin = turn_cos_sin((slot - half) * shift_x[:, :, None], period)
    both = turn_cos_sin(shift_y + shift_x, 2 * SUBPIX)[0][:, :, None]
    only_y = turn_cos_sin(shift_y, 2 * SUBPIX)[0][:, :, None]
    only_x = turn_cos_sin(shift_x, 2 * SUBPIX)[0][:, :, None]
    zero = slot == 0
    same_re = jnp.where(zero, only_y, 2.0 * both * col_cos) * scale
    same_im = jnp.where(zero, both, 2.0 * both * col_cos) * scale
    cross = jnp.where(zero, 0.0, 2.0 * both * col_sin) * scale
    first_re = jnp.where(zero, 1.0, 2.0 * only_x * col_cos) * scale
    first_im = jnp.where(zero, only_x, 2.0 * only_x * col_cos) * scale
    first_cross = jnp.where(zero, 0.0, 2.0 * only_x * col_sin) * scale
    lanes = jnp.concatenate
    same = lanes([same_re, same_im], axis=2)
    swap = lanes([cross, -cross], axis=2)
    first_same = lanes([first_re, first_im], axis=2)
    first_swap = lanes([first_cross, -first_cross], axis=2)
    return row_cos, row_sin, same, swap, first_same, first_swap


def local(images, rate_vectors, epoch_times):
    loc_epochs, loc_rows, length = images.shape
    row_count = lax.axis_size("row")
    epoch_count = lax.axis_size("epoch")
    devices = row_count * epoch_count
    place = lax.axis_index("row") * epoch_count + lax.axis_index("epoch")
    lanes = length // devices
    slots = lanes // 2
    half = length // 2
    rates = rate_vectors.shape[0]
    table = real_table(length)
    lane_table = table[lane_order(length, devices)]
    rowwise = jnp.asarray(np.ascontiguousarray(lane_table.T))
    inverse = jnp.asarray(lane_table).reshape(devices, lanes, length)
    forward = jnp.asarray(table)
    spectrum = jnp.einsum("erc,cl->erl", images, rowwise, preferred_element_type=jnp.float32)
    spectrum = spectrum.astype(jnp.bfloat16).reshape(loc_epochs, loc_rows, devices, lanes)
    sent = spectrum.transpose(2, 0, 1, 3)
    got = lax.all_to_all(sent, ("row", "epoch"), split_axis=0, concat_axis=0, tiled=True)
    got = got.reshape(row_count, epoch_count * loc_epochs, loc_rows, lanes)
    pairs = jnp.einsum(
        "uir,ierl->eul",
        forward.reshape(length, row_count, loc_rows),
        got,
        preferred_element_type=jnp.float32,
    )
    row_cos, row_sin, same, swap, first_same, first_swap = coefficients(
        rate_vectors, epoch_times, place * slots, slots, length
    )
    even, odd = pairs[:, :half], pairs[:, half:]
    swapped = lambda a: jnp.concatenate([a[..., slots:], a[..., :slots]], axis=-1)
    row_cos, row_sin = row_cos[..., None], row_sin[..., None]
    moved_even = row_cos * even[None] + row_sin * odd[None]
    moved_odd = row_cos * odd[None] - row_sin * even[None]
    first = (jnp.arange(half) == 0)[None, None, :, None]
    same_even = jnp.where(first, first_same[:, :, None], same[:, :, None])
    swap_even = jnp.where(first, first_swap[:, :, None], swap[:, :, None])
    sum_even = jnp.sum(same_even * moved_even + swap_even * swapped(moved_even), axis=1)
    sum_odd = jnp.sum(same[:, :, None] * moved_odd + swap[:, :, None] * swapped(moved_odd), axis=1)
    stacked = jnp.concatenate([sum_even, sum_odd], axis=1).astype(jnp.bfloat16)
    back = jnp.einsum("ur,kul->krl", forward, stacked, preferred_element_type=jnp.float32)
    back = back.astype(jnp.bfloat16)
    back = back.reshape(epoch_count, rates // epoch_count, row_count, loc_rows, lanes)
    back = back.transpose(2, 0, 1, 3, 4).reshape(devices, rates // epoch_count, loc_rows, lanes)
    returned = lax.all_to_all(back, ("row", "epoch"), split_axis=0, concat_axis=0, tiled=True)
    return jnp.einsum("dkrl,dlc->krc", returned, inverse, preferred_element_type=jnp.float32)


def solution(mesh):
    in_specs = (P(("group", "epoch"), "row", None), P(), P())
    out_specs = P(("group", "epoch"), "row", None)
    return jax.shard_map(local, mesh=mesh, in_specs=in_specs, out_specs=out_specs, check_vma=False)
```

time: 458 us -> 126 us (0.28)
  the two profiles are of different devices: /device:TPU:0 before, /device:TPU:11 now
where the time goes in v1:
time: 126 us; the launch traced here: 125 us
  waiting for transfers between devices  46.3 us (37%)
  blocking collectives  29.5 us (23%)
  matrix products  29.3 us (23%)
  local copies, waits for them, and re-layouts  8.78 us (7%)
  starting transfers between devices  6.55 us (5%)
  other arithmetic  4.05 us (3%)
    all_to_all x1, waiting for transfers between devices, local(): lax.all_to_all(sent, ('row', 'epoch'), split_axis=0, concat_axis=0, tiled...  46.3 us
    all_to_all x1, blocking collectives, local(): lax.all_to_all(back, ('row', 'epoch'), split_axis=0, concat_axis=0, tiled...  29.5 us
    dot_general x1, matrix products, local(): jnp.einsum('erc,cl->erl', images, rowwise, preferred_element_type=jnp.flo...  9.15 us
    dot_general x1, matrix products, local(): jnp.einsum('uir,ierl->eul', forward.reshape(length, row_count, loc_rows),...  8.07 us
    all_to_all x1, starting transfers between devices, local(): lax.all_to_all(sent, ('row', 'epoch'), split_axis=0, concat_axis=0, tiled...  6.55 us
    dot_general x1, matrix products, local(): jnp.einsum('dkrl,dlc->krc', returned, inverse, preferred_element_type=jnp...  6.31 us
    dot_general x1, matrix products, local(): jnp.einsum('ur,kul->krl', forward, stacked, preferred_element_type=jnp.fl...  5.75 us
    reshape x1, local copies, waits for them, and re-layouts, local(): spectrum.astype(jnp.bfloat16).reshape(loc_epochs, loc_rows, devices, lanes)  3.95 us
  transfers between devices with their start and end apart: 1, of which 1 were waited for; matrix products, arithmetic and copies ran while one was open for 1% of the time, Pallas kernels for 0%

profile of v1, /device:TPU:11, one launch (start us, length us, event | category | flops | bytes accessed | tf_op | source)
XLA Modules:
  0.0 124.6 jit_solution(73334010471328594)
XLA Ops:
  0.0 0.0 copy-start
  0.0 1.6 %copy-done = bf16[2,256,2048]{2,1,0:T(8,128)(2,1)S(1)} copy-done((bf16[2,256,2048]{2,1,0:T(8,128)(2,1)S(1)}, bf16[2,256,2048]{2,1,0:T(8,128)(2,1)}, u32[]{:S(2)}) %copy-start) | copy-done | bytes 2097176
  1.6 9.2 %convolution_convert_fusion = bf16[2048,2,256]{2,0,1:T(8,128)(2,1)} fusion(bf16[2048,2048,1]{0,1,2:T(8,128)(2,1)} %constant.102, bf16[2,256,2048]{2,1,0:T(8,128)(2,1)S(1)} %copy-done), kind=kOutput, calls=%fused_computation.9 | convolution fusion | flops 4296015872 | bytes 12582912 | tf_op jit(solution)/shard_map/erc,cl->erl/dot_general | solution.py:82
  10.7 4.0 %copy.20 = bf16[2,256,16,128]{3,1,0,2:T(8,128)(2,1)} copy(bf16[2,256,16,128]{1,3,2,0:T(8,128)(2,1)} %bitcast.42) | data formatting | bytes 4194304 | tf_op jit(solution)/shard_map/reshape | solution.py:83
  14.7 6.6 %all-to-all-start = ((bf16[16,2,256,128]{3,2,1,0:T(8,128)(2,1)}), bf16[16,2,256,128]{3,2,1,0:T(8,128)(2,1)S(1)}, u32[]{:S(2)}, u32[]{:S(2)}) async-start(bf16[16,2,256,128]{3,2,1,0:T(8,128)(2,1)} %bitcast.3), calls=%async_computation | async-start | bytes 4194304 | tf_op jit(solution)/shard_map/all_to_all | solution.py:85
  21.3 0.0 copy-done.2
  21.3 0.2 slice_reduce_fusion.1
  21.5 0.1 and_select_fusion.4
  21.6 0.1 fusion.19
  21.7 0.1 select_multiply_fusion.5
  21.9 0.1 pad_maximum_fusion.2
  21.9 0.1 pad_maximum_fusion.4
  22.0 0.4 multiply_select_fusion.2
  22.4 46.3 %all-to-all-done = bf16[16,2,256,128]{3,2,1,0:T(8,128)(2,1)S(1)} async-done(((bf16[16,2,256,128]{3,2,1,0:T(8,128)(2,1)}), bf16[16,2,256,128]{3,2,1,0:T(8,128)(2,1)S(1)}, u32[]{:S(2)}, u32[]{:S(2)}) %all-to-all-start) | async-done | bytes 2097184 | tf_op jit(solution)/shard_map/all_to_all | solution.py:85
  68.7 8.1 %convolution_bitcast_fusion = f32[4,2048,128]{1,2,0:T(8,128)S(1)} fusion(bf16[2048,8,256,1]{2,0,3,1:T(8,128)(2,1)} %constant.103, bf16[8,4,256,128]{3,2,1,0:T(8,128)(2,1)S(1)} %bitcast.41), kind=kOutput, calls=%fused_computation.8 | convolution fusion | flops 4294967296 | bytes 14680064 | tf_op jit(solution)/shard_map/uir,ierl->eul/dot_general | solution.py:87
  76.8 0.3 fusion.37
  77.1 1.2 multiply_subtract_fusion
  78.3 1.4 %fusion.35 = (f32[2,4,1024,64]{2,3,1,0:T(8,128)S(1)}, f32[2,4,1024,64]{2,3,1,0:T(8,128)S(1)}, f32[2,4,1024,64]{2,3,1,0:T(8,128)S(1)}, f32[2,4,1024,64]{2,3,1,0:T(8,128)S(1)}) fusion(f32[2,4,1024,128]{2,3,1,0:T(8,128)S(1)} %get-tuple-element.11, f32[2,4,1024,128]{2,3,1,0:T(8,128)S(1)} %get-tuple-element.12), kind=kLoop, calls=%fused_computation.89 | loop fusion | bytes 16777216 | tf_op jit(solution)/shard_map/slice | solution.py:97
  79.7 2.0 %fusion.1 = (bf16[2,1024,128]{1,2,0:T(8,128)(2,1)S(1)}, bf16[2,1024,128]{1,2,0:T(8,128)(2,1)S(1)}) fusion(f32[2,4,1024,64]{2,3,1,0:T(8,128)S(1)} %get-tuple-element.40, f32[2,4,1024,64]{2,3,1,0:T(8,128)S(1)} %get-tuple-element.41, f32[2,4,1024,128]{2,3,1,0:T(8,128)S(1)} %get-tuple-element.12, f32[2,4,128]{2,1,0:T(4,128)S(1)} %get-tuple-element.45, ...), kind=kLoop, calls=%fused_computation.2 | loop fusion | flops 12058624 | bytes 17843200 | tf_op jit(solution)/shard_map/reduce_sum | solution.py:104
  81.7 5.7 %convolution_convert_fusion.1 = bf16[2,128,2048]{2,1,0:T(8,128)(2,1)S(1)} fusion(bf16[2048,2048,1]{1,0,2:T(8,128)(2,1)} %constant.104, bf16[2,1024,128]{1,2,0:T(8,128)(2,1)S(1)} %get-tuple-element.6, bf16[2,1024,128]{1,2,0:T(8,128)(2,1)S(1)} %get-tuple-element.5), kind=kOutput, calls=%fused_computation.11 | convolution fusion | flops 2150105088 | bytes 10485760 | tf_op jit(solution)/shard_map/ur,kul->krl/dot_general | solution.py:107
  87.5 0.3 copy.31
  87.8 1.0 copy.26
  88.8 29.5 %all_to_all.10 = bf16[16,1,256,128]{3,2,1,0:T(8,128)(2,1)S(1)} all-to-all(bf16[16,1,256,128]{3,2,1,0:T(8,128)(2,1)S(1)} %bitcast.40), channel_id=1, replica_groups=mesh['group'=2,'row'=8,'epoch'=2] {'row','epoch'}, dimensions={0} | all-to-all | bytes 2097152 | tf_op jit(solution)/shard_map/all_to_all | solution.py:111
  118.3 6.3 %convolution_bitcast_fusion.1 = f32[1,256,2048]{2,1,0:T(8,128)} fusion(bf16[16,128,2048]{2,1,0:T(8,128)(2,1)} %constant.101, bf16[16,1,256,128]{3,2,1,0:T(8,128)(2,1)S(1)} %all_to_all.10), kind=kOutput, calls=%fused_computation.10 | convolution fusion | flops 2147483648 | bytes 11534336 | tf_op jit(solution)/shard_map/dkrl,dlc->krc/dot_general | solution.py:112
  (9 shorter events, 0.0 us)
Async XLA Ops:
  0.0 1.6 %copy-start = (bf16[2,256,2048]{2,1,0:T(8,128)(2,1)S(1)}, bf16[2,256,2048]{2,1,0:T(8,128)(2,1)}, u32[]{:S(2)}) copy-start(bf16[2,256,2048]{2,1,0:T(8,128)(2,1)} %param.6) | copy-start | bytes 6291460
  10.7 10.6 %copy-start.2 = (s32[2,2]{1,0:T(2,128)S(1)}, s32[2,2]{1,0:T(2,128)}, u32[]{:S(2)}) copy-start(s32[2,2]{1,0:T(2,128)} %param.7) | copy-start | bytes 52
  10.7 10.8 %copy-start.3 = (s32[4]{0:T(128)S(1)}, s32[4]{0:T(128)}, u32[]{:S(2)}) copy-start(s32[4]{0:T(128)} %param.8) | copy-start | bytes 52
  14.7 54.0 %all-to-all-start = ((bf16[16,2,256,128]{3,2,1,0:T(8,128)(2,1)}), bf16[16,2,256,128]{3,2,1,0:T(8,128)(2,1)S(1)}, u32[]{:S(2)}, u32[]{:S(2)}) async-start(bf16[16,2,256,128]{3,2,1,0:T(8,128)(2,1)} %bitcast.3), calls=%async_computation | async-start | bytes 4194304 | tf_op jit(solution)/shard_map/all_to_all | solution.py:85
  118.3 6.3 %copy-start.1 = (bf16[2,256,2048]{2,1,0:T(8,128)(2,1)S(1)}, bf16[2,256,2048]{2,1,0:T(8,128)(2,1)}, u32[]{:S(2)}) copy-start(bf16[2,256,2048]{2,1,0:T(8,128)(2,1)} %param.6) | copy-start | bytes 6291460

commit v2 on v1

--- a/solution.py
+++ b/solution.py
@@ -79,37 +79,59 @@
     rowwise = jnp.asarray(np.ascontiguousarray(lane_table.T))
     inverse = jnp.asarray(lane_table).reshape(devices, lanes, length)
     forward = jnp.asarray(table)
-    spectrum = jnp.einsum("erc,cl->erl", images, rowwise, preferred_element_type=jnp.float32)
-    spectrum = spectrum.astype(jnp.bfloat16).reshape(loc_epochs, loc_rows, devices, lanes)
-    sent = spectrum.transpose(2, 0, 1, 3)
-    got = lax.all_to_all(sent, ("row", "epoch"), split_axis=0, concat_axis=0, tiled=True)
-    got = got.reshape(row_count, epoch_count * loc_epochs, loc_rows, lanes)
-    pairs = jnp.einsum(
-        "uir,ierl->eul",
-        forward.reshape(length, row_count, loc_rows),
-        got,
-        preferred_element_type=jnp.float32,
-    )
+    table_blocks = forward.reshape(length, row_count, loc_rows)
+    parts = []
+    for epoch in range(loc_epochs):
+        spectrum = jnp.einsum(
+            "rc,cl->rl", images[epoch], rowwise, preferred_element_type=jnp.float32
+        )
+        sent = spectrum.astype(jnp.bfloat16).reshape(loc_rows, devices, lanes).transpose(1, 0, 2)
+        got = lax.all_to_all(sent, ("row", "epoch"), split_axis=0, concat_axis=0, tiled=True)
+        got = got.reshape(row_count, epoch_count, loc_rows, lanes)
+        parts.append(
+            jnp.einsum("uir,ijrl->jul", table_blocks, got, preferred_element_type=jnp.float32)
+        )
     row_cos, row_sin, same, swap, first_same, first_swap = coefficients(
         rate_vectors, epoch_times, place * slots, slots, length
     )
-    even, odd = pairs[:, :half], pairs[:, half:]
     swapped = lambda a: jnp.concatenate([a[..., slots:], a[..., :slots]], axis=-1)
     row_cos, row_sin = row_cos[..., None], row_sin[..., None]
-    moved_even = row_cos * even[None] + row_sin * odd[None]
-    moved_odd = row_cos * odd[None] - row_sin * even[None]
-    first = (jnp.arange(half) == 0)[None, None, :, None]
-    same_even = jnp.where(first, first_same[:, :, None], same[:, :, None])
-    swap_even = jnp.where(first, first_swap[:, :, None], swap[:, :, None])
-    sum_even = jnp.sum(same_even * moved_even + swap_even * swapped(moved_even), axis=1)
-    sum_odd = jnp.sum(same[:, :, None] * moved_odd + swap[:, :, None] * swapped(moved_odd), axis=1)
+    swap, first_swap = swapped(swap), swapped(first_swap)
+    sums = [0.0] * 6
+    for epoch, pairs in enumerate(parts):
+        for source in range(epoch_count):
+            at = source * loc_epochs + epoch
+            even, odd = pairs[source, :half][None], pairs[source, half:][None]
+            moved_even = row_cos[:, at] * even + row_sin[:, at] * odd
+            moved_odd = row_cos[:, at] * odd - row_sin[:, at] * even
+            terms = (
+                same[:, at, None] * moved_even,
+                swap[:, at, None] * moved_even,
+                same[:, at, None] * moved_odd,
+                swap[:, at, None] * moved_odd,
+                first_same[:, at, None] * even[:, :1],
+                first_swap[:, at, None] * even[:, :1],
+            )
+            sums = [total + term for total, term in zip(sums, terms)]
+    first = (jnp.arange(half) == 0)[None, :, None]
+    sum_even = jnp.where(first, sums[4] + swapped(sums[5]), sums[0] + swapped(sums[1]))
+    sum_odd = sums[2] + swapped(sums[3])
     stacked = jnp.concatenate([sum_even, sum_odd], axis=1).astype(jnp.bfloat16)
-    back = jnp.einsum("ur,kul->krl", forward, stacked, preferred_element_type=jnp.float32)
-    back = back.astype(jnp.bfloat16)
-    back = back.reshape(epoch_count, rates // epoch_count, row_count, loc_rows, lanes)
-    back = back.transpose(2, 0, 1, 3, 4).reshape(devices, rates // epoch_count, loc_rows, lanes)
-    returned = lax.all_to_all(back, ("row", "epoch"), split_axis=0, concat_axis=0, tiled=True)
-    return jnp.einsum("dkrl,dlc->krc", returned, inverse, preferred_element_type=jnp.float32)
+    half_rows = loc_rows // 2
+    halves = table.reshape(length, row_count, 2, half_rows)
+    results = []
+    for part in range(2):
+        columns = jnp.asarray(np.ascontiguousarray(halves[:, :, part]).reshape(length, -1))
+        back = jnp.einsum("ur,kul->krl", columns, stacked, preferred_element_type=jnp.float32)
+        back = back.astype(jnp.bfloat16)
+        back = back.reshape(epoch_count, rates // epoch_count, row_count, half_rows, lanes)
+        back = back.transpose(2, 0, 1, 3, 4)
+        back = back.reshape(devices, rates // epoch_count, half_rows, lanes)
+        returned = lax.all_to_all(back, ("row", "epoch"), split_axis=0, concat_axis=0, tiled=True)
+        results.append(
+            jnp.einsum("dkrl,dlc->krc", returned, inverse, preferred_element_type=jnp.float32)
+        )
+    return jnp.concatenate(results, axis=1)
 
 
 def solution(mesh):

time: 126 us -> 129 us (1.024)
  blocking collectives: 29.5 us -> 0 us
  starting transfers between devices: 6.55 us -> 21.4 us
  matrix products: 29.3 us -> 38.5 us
  waiting for transfers between devices: 46.3 us -> 52.8 us
  other arithmetic: 4.05 us -> 7.21 us
  local copies, waits for them, and re-layouts: 8.78 us -> 6.93 us
    all_to_all x1 -> x0, blocking collectives: 29.5 us -> none  [local(): lax.all_to_all(back, ('row', 'epoch'), split_axis=0, concat_axis=0, tiled...]
    all_to_all x0 -> x2, waiting for transfers between devices: none -> 17.7 us  [local(): lax.all_to_all(back, ('row', 'epoch'), split_axis=0, concat_axis=0, tiled...]
    all_to_all x1 -> x2, waiting for transfers between devices: 46.3 us -> 35.1 us  [local(): lax.all_to_all(sent, ('row', 'epoch'), split_axis=0, concat_axis=0, tiled...]
    all_to_all x0 -> x2, starting transfers between devices: none -> 9.92 us  [local(): lax.all_to_all(back, ('row', 'epoch'), split_axis=0, concat_axis=0, tiled...]
    dot_general x3 -> x6, matrix products: 23 us -> 29.1 us  [the longest x2 12.5 us: local(): jnp.einsum('rc,cl->rl', images[epoch], rowwise, preferred_element_type=jn...]
    all_to_all x1 -> x2, starting transfers between devices: 6.55 us -> 11.5 us  [local(): lax.all_to_all(sent, ('row', 'epoch'), split_axis=0, concat_axis=0, tiled...]
    dot_general x1 -> x2, matrix products: 6.31 us -> 9.37 us  [local(): jnp.einsum('dkrl,dlc->krc', returned, inverse, preferred_element_type=jnp...]
    another operation x0 -> x2, other arithmetic: none -> 2.37 us
  transfers between devices with their start and end apart: 1 -> 4, of which waited for: 1 -> 4; matrix products, arithmetic and copies ran while one was open for 1% -> 19% of each run, Pallas kernels for 0% -> 0%
where the time goes in v2:
time: 129 us; the launch traced here: 127 us
  waiting for transfers between devices  52.8 us (41%)
  matrix products  38.5 us (30%)
  starting transfers between devices  21.4 us (17%)
  other arithmetic  7.21 us (6%)
  local copies, waits for them, and re-layouts  6.93 us (5%)
    all_to_all x2, waiting for transfers between devices, local(): lax.all_to_all(sent, ('row', 'epoch'), split_axis=0, concat_axis=0, tiled...  35.1 us
    all_to_all x2, waiting for transfers between devices, local(): lax.all_to_all(back, ('row', 'epoch'), split_axis=0, concat_axis=0, tiled...  17.7 us
    dot_general x2, matrix products, local(): jnp.einsum('rc,cl->rl', images[epoch], rowwise, preferred_element_type=jn...  12.5 us
    dot_general x2, matrix products, local(): jnp.einsum('uir,ijrl->jul', table_blocks, got, preferred_element_type=jnp...  11.9 us
    all_to_all x2, starting transfers between devices, local(): lax.all_to_all(sent, ('row', 'epoch'), split_axis=0, concat_axis=0, tiled...  11.5 us
    all_to_all x2, starting transfers between devices, local(): lax.all_to_all(back, ('row', 'epoch'), split_axis=0, concat_axis=0, tiled...  9.92 us
    dot_general x2, matrix products, local(): jnp.einsum('dkrl,dlc->krc', returned, inverse, preferred_element_type=jnp...  9.37 us
    dot_general x2, matrix products, local(): jnp.einsum('ur,kul->krl', columns, stacked, preferred_element_type=jnp.fl...  4.74 us
  transfers between devices with their start and end apart: 4, of which 4 were waited for; matrix products, arithmetic and copies ran while one was open for 19% of the time, Pallas kernels for 0%

profile of v2, /device:TPU:11, one launch (start us, length us, event | category | flops | bytes accessed | tf_op | source)
XLA Modules:
  0.0 127.1 jit_solution(1785927886281679024)
XLA Ops:
  0.0 6.2 %convolution_convert_fusion = bf16[2048,256]{1,0:T(8,128)(2,1)S(1)} fusion(bf16[2048,2048]{1,0:T(8,128)(2,1)} %constant.100.clone, bf16[2,256,2048]{2,1,0:T(8,128)(2,1)} %param.8), kind=kOutput, calls=%fused_computation.2 | convolution fusion | flops 2148007936 | bytes 10485760 | tf_op jit(solution)/shard_map/rc,cl->rl/dot_general | solution.py:85
  6.2 1.3 %copy.19 = bf16[256,16,128]{2,0,1:T(8,128)(2,1)} copy(bf16[256,16,128]{0,2,1:T(8,128)(2,1)S(1)} %bitcast.125) | data formatting | bytes 2097152 | tf_op jit(solution)/shard_map/reshape | solution.py:88
  7.5 6.6 %all-to-all-start.1 = ((bf16[16,256,128]{2,1,0:T(8,128)(2,1)}), bf16[16,256,128]{2,1,0:T(8,128)(2,1)S(1)}, u32[]{:S(2)}, u32[]{:S(2)}) async-start(bf16[16,256,128]{2,1,0:T(8,128)(2,1)} %bitcast.13), calls=%async_computation.1 | async-start | bytes 2097152 | tf_op jit(solution)/shard_map/all_to_all | solution.py:89
  14.1 6.3 %convolution_convert_fusion.1 = bf16[2048,256]{1,0:T(8,128)(2,1)S(1)} fusion(bf16[2048,2048]{1,0:T(8,128)(2,1)} %constant.100.clone, bf16[2,256,2048]{2,1,0:T(8,128)(2,1)} %param.8), kind=kOutput, calls=%fused_computation.3 | convolution fusion | flops 2148007936 | bytes 10485760 | tf_op jit(solution)/shard_map/rc,cl->rl/dot_general | solution.py:85
  20.4 1.3 %copy.17 = bf16[256,16,128]{2,0,1:T(8,128)(2,1)} copy(bf16[256,16,128]{0,2,1:T(8,128)(2,1)S(1)} %bitcast.124) | data formatting | bytes 2097152 | tf_op jit(solution)/shard_map/reshape | solution.py:88
  21.9 17.0 %all-to-all-done.1 = bf16[16,256,128]{2,1,0:T(8,128)(2,1)S(1)} async-done(((bf16[16,256,128]{2,1,0:T(8,128)(2,1)}), bf16[16,256,128]{2,1,0:T(8,128)(2,1)S(1)}, u32[]{:S(2)}, u32[]{:S(2)}) %all-to-all-start.1) | async-done | bytes 1048608 | tf_op jit(solution)/shard_map/all_to_all | solution.py:89
  38.9 4.9 %all-to-all-start = ((bf16[16,256,128]{2,1,0:T(8,128)(2,1)}), bf16[16,256,128]{2,1,0:T(8,128)(2,1)}, u32[]{:S(2)}, u32[]{:S(2)}) async-start(bf16[16,256,128]{2,1,0:T(8,128)(2,1)} %bitcast.3), calls=%async_computation | async-start | bytes 2097152 | tf_op jit(solution)/shard_map/all_to_all | solution.py:89
  45.0 5.8 %convolution_bitcast_fusion = f32[2,2048,128]{1,2,0:T(8,128)S(1)} fusion(bf16[8,2,256,128]{3,2,1,0:T(8,128)(2,1)S(1)} %bitcast.123, bf16[2048,8,256,1]{2,0,3,1:T(8,128)(2,1)} %constant.108), kind=kOutput, calls=%fused_computation | convolution fusion | flops 2147483648 | bytes 11534336 | tf_op jit(solution)/shard_map/uir,ijrl->jul/dot_general | solution.py:92
  50.8 18.1 %all-to-all-done = bf16[16,256,128]{2,1,0:T(8,128)(2,1)} async-done(((bf16[16,256,128]{2,1,0:T(8,128)(2,1)}), bf16[16,256,128]{2,1,0:T(8,128)(2,1)}, u32[]{:S(2)}, u32[]{:S(2)}) %all-to-all-start) | async-done | bytes 1048608 | tf_op jit(solution)/shard_map/all_to_all | solution.py:89
  68.9 6.1 %convolution_bitcast_fusion.1 = f32[2,2048,128]{1,2,0:T(8,128)S(1)} fusion(bf16[8,2,256,128]{3,2,1,0:T(8,128)(2,1)} %bitcast.4, bf16[2048,8,256,1]{2,0,3,1:T(8,128)(2,1)} %constant.108), kind=kOutput, calls=%fused_computation.1 | convolution fusion | flops 2147483648 | bytes 11534336 | tf_op jit(solution)/shard_map/uir,ijrl->jul/dot_general | solution.py:92
  76.5 1.1 multiply_add_fusion
  78.0 1.2 fusion.2
  79.2 1.2 fusion.1
  81.4 1.3 %convolution_convert_fusion.3 = bf16[2,128,1024]{2,1,0:T(8,128)(2,1)S(1)} fusion(bf16[2048,1024,1]{1,0,2:T(8,128)(2,1)S(1)} %copy-done.2, bf16[2,1024,128]{1,2,0:T(8,128)(2,1)S(1)} %fusion.2, bf16[2,1024,128]{1,2,0:T(8,128)(2,1)S(1)} %fusion.1), kind=kOutput, calls=%fused_computation.8 | convolution fusion | flops 1076101120 | bytes 5767168 | tf_op jit(solution)/shard_map/ur,kul->krl/dot_general | solution.py:125
  82.8 1.1 copy.21
  83.9 4.9 %all-to-all-start.2 = ((bf16[16,1,128,128]{3,2,1,0:T(8,128)(2,1)}), bf16[16,1,128,128]{3,2,1,0:T(8,128)(2,1)S(1)}, u32[]{:S(2)}, u32[]{:S(2)}) async-start(bf16[16,1,128,128]{3,2,1,0:T(8,128)(2,1)} %bitcast.47), calls=%async_computation.2 | async-start | bytes 1048576 | tf_op jit(solution)/shard_map/all_to_all | solution.py:130
  88.8 3.5 %convolution_convert_fusion.2 = bf16[2,128,1024]{2,1,0:T(8,128)(2,1)S(1)} fusion(bf16[2048,1024,1]{1,0,2:T(8,128)(2,1)} %constant.110, bf16[2,1024,128]{1,2,0:T(8,128)(2,1)S(1)} %fusion.2, bf16[2,1024,128]{1,2,0:T(8,128)(2,1)S(1)} %fusion.1), kind=kOutput, calls=%fused_computation.7 | convolution fusion | flops 1076101120 | bytes 5767168 | tf_op jit(solution)/shard_map/ur,kul->krl/dot_general | solution.py:125
  92.4 1.1 copy.22
  93.5 8.9 %all-to-all-done.2 = bf16[16,1,128,128]{3,2,1,0:T(8,128)(2,1)S(1)} async-done(((bf16[16,1,128,128]{3,2,1,0:T(8,128)(2,1)}), bf16[16,1,128,128]{3,2,1,0:T(8,128)(2,1)S(1)}, u32[]{:S(2)}, u32[]{:S(2)}) %all-to-all-start.2) | async-done | bytes 524320 | tf_op jit(solution)/shard_map/all_to_all | solution.py:130
  102.4 5.0 %all-to-all-start.3 = ((bf16[16,1,128,128]{3,2,1,0:T(8,128)(2,1)}), bf16[16,1,128,128]{3,2,1,0:T(8,128)(2,1)S(1)}, u32[]{:S(2)}, u32[]{:S(2)}) async-start(bf16[16,1,128,128]{3,2,1,0:T(8,128)(2,1)} %bitcast.54), calls=%async_computation.3 | async-start | bytes 1048576 | tf_op jit(solution)/shard_map/all_to_all | solution.py:130
  107.4 4.7 %convolution_bitcast_fusion.3 = f32[1,128,2048]{2,1,0:T(8,128)S(1)} fusion(bf16[16,128,2048]{2,1,0:T(8,128)(2,1)} %constant.107, bf16[16,1,128,128]{3,2,1,0:T(8,128)(2,1)S(1)} %all-to-all-done.2), kind=kOutput, calls=%fused_computation.5 | convolution fusion | flops 1073741824 | bytes 9961472 | tf_op jit(solution)/shard_map/dkrl,dlc->krc/dot_general | solution.py:132
  112.1 8.8 %all-to-all-done.3 = bf16[16,1,128,128]{3,2,1,0:T(8,128)(2,1)S(1)} async-done(((bf16[16,1,128,128]{3,2,1,0:T(8,128)(2,1)}), bf16[16,1,128,128]{3,2,1,0:T(8,128)(2,1)S(1)}, u32[]{:S(2)}, u32[]{:S(2)}) %all-to-all-start.3) | async-done | bytes 524320 | tf_op jit(solution)/shard_map/all_to_all | solution.py:130
  121.0 4.6 %convolution_bitcast_fusion.2 = f32[1,128,2048]{2,1,0:T(8,128)S(1)} fusion(bf16[16,128,2048]{2,1,0:T(8,128)(2,1)} %constant.107, bf16[16,1,128,128]{3,2,1,0:T(8,128)(2,1)S(1)} %all-to-all-done.3), kind=kOutput, calls=%fused_computation.4 | convolution fusion | flops 1073741824 | bytes 9961472 | tf_op jit(solution)/shard_map/dkrl,dlc->krc/dot_general | solution.py:132
  125.6 1.5 %pad_maximum_fusion = f32[1,256,2048]{2,1,0:T(8,128)} fusion(f32[1,128,2048]{2,1,0:T(8,128)S(1)} %convolution_bitcast_fusion.2, f32[1,128,2048]{2,1,0:T(8,128)S(1)} %convolution_bitcast_fusion.3), kind=kLoop, calls=%fused_computation.6 | loop fusion | flops 524288 | bytes 4194304 | tf_op jit(solution)/shard_map/concatenate | solution.py:134
  (27 shorter events, 4.3 us)
Async XLA Ops:
  7.5 31.4 %all-to-all-start.1 = ((bf16[16,256,128]{2,1,0:T(8,128)(2,1)}), bf16[16,256,128]{2,1,0:T(8,128)(2,1)S(1)}, u32[]{:S(2)}, u32[]{:S(2)}) async-start(bf16[16,256,128]{2,1,0:T(8,128)(2,1)} %bitcast.13), calls=%async_computation.1 | async-start | bytes 2097152 | tf_op jit(solution)/shard_map/all_to_all | solution.py:89
  14.1 7.7 %copy-start = (s32[2,2]{1,0:T(2,128)S(1)}, s32[2,2]{1,0:T(2,128)}, u32[]{:S(2)}) copy-start(s32[2,2]{1,0:T(2,128)} %param.9) | copy-start | bytes 52
  20.4 23.5 %copy-start.1 = (s32[4]{0:T(128)S(1)}, s32[4]{0:T(128)}, u32[]{:S(2)}) copy-start(s32[4]{0:T(128)} %param.10) | copy-start | bytes 52
  38.9 29.9 %all-to-all-start = ((bf16[16,256,128]{2,1,0:T(8,128)(2,1)}), bf16[16,256,128]{2,1,0:T(8,128)(2,1)}, u32[]{:S(2)}, u32[]{:S(2)}) async-start(bf16[16,256,128]{2,1,0:T(8,128)(2,1)} %bitcast.3), calls=%async_computation | async-start | bytes 2097152 | tf_op jit(solution)/shard_map/all_to_all | solution.py:89
  79.2 2.2 %copy-start.2 = (bf16[2048,1024,1]{1,0,2:T(8,128)(2,1)S(1)}, bf16[2048,1024,1]{1,0,2:T(8,128)(2,1)}, u32[]{:S(2)}) copy-start(bf16[2048,1024,1]{1,0,2:T(8,128)(2,1)} %constant.109) | copy-start | bytes 12582916
  83.9 18.5 %all-to-all-start.2 = ((bf16[16,1,128,128]{3,2,1,0:T(8,128)(2,1)}), bf16[16,1,128,128]{3,2,1,0:T(8,128)(2,1)S(1)}, u32[]{:S(2)}, u32[]{:S(2)}) async-start(bf16[16,1,128,128]{3,2,1,0:T(8,128)(2,1)} %bitcast.47), calls=%async_computation.2 | async-start | bytes 1048576 | tf_op jit(solution)/shard_map/all_to_all | solution.py:130
  102.4 18.6 %all-to-all-start.3 = ((bf16[16,1,128,128]{3,2,1,0:T(8,128)(2,1)}), bf16[16,1,128,128]{3,2,1,0:T(8,128)(2,1)S(1)}, u32[]{:S(2)}, u32[]{:S(2)}) async-start(bf16[16,1,128,128]{3,2,1,0:T(8,128)(2,1)} %bitcast.54), calls=%async_computation.3 | async-start | bytes 1048576 | tf_op jit(solution)/shard_map/all_to_all | solution.py:130

commit v3 on v1

--- a/solution.py
+++ b/solution.py
@@ -6,6 +6,8 @@
 import ml_dtypes
 import numpy as np
 from jax import lax
+from jax.experimental import pallas as pl
+from jax.experimental.pallas import tpu as pltpu
 from jax.sharding import PartitionSpec as P
 
 SUBPIX = 16
@@ -64,6 +66,57 @@
     return row_cos, row_sin, same, swap, first_same, first_swap
 
 
+def exchange_kernel(rows, cores, src, dst, send_sem, recv_sem, own_sem):
+    count = rows * cores
+    me = lax.axis_index("row") * cores + lax.axis_index("epoch")
+    barrier = pltpu.get_barrier_semaphore()
+
+    def peer(step):
+        other = lax.rem(me + step, count)
+        return other, {"row": lax.div(other, cores), "epoch": lax.rem(other, cores)}
+
+    for step in range(1, count):
+        pl.semaphore_signal(
+            barrier, inc=1, device_id=peer(step)[1], device_id_type=pl.DeviceIdType.MESH
+        )
+    own = pltpu.make_async_copy(src.at[me], dst.at[me], own_sem)
+    own.start()
+    pl.semaphore_wait(barrier, count - 1)
+    copies = []
+    for step in range(1, count):
+        other, device = peer(step)
+        copy = pltpu.make_async_remote_copy(
+            src_ref=src.at[other],
+            dst_ref=dst.at[me],
+            send_sem=send_sem.at[step],
+            recv_sem=recv_sem.at[step],
+            device_id=device,
+            device_id_type=pl.DeviceIdType.MESH,
+        )
+        copy.start()
+        copies.append(copy)
+    own.wait()
+    for copy in copies:
+        copy.wait()
+
+
+def exchange(blocks, rows, cores, identity):
+    if blocks.shape[-1] % 128 or blocks.shape[-2] % 16:
+        return lax.all_to_all(blocks, ("row", "epoch"), split_axis=0, concat_axis=0, tiled=True)
+    return pl.pallas_call(
+        functools.partial(exchange_kernel, rows, cores),
+        out_shape=jax.ShapeDtypeStruct(blocks.shape, blocks.dtype),
+        in_specs=[pl.BlockSpec(memory_space=pl.ANY)],
+        out_specs=pl.BlockSpec(memory_space=pl.ANY),
+        scratch_shapes=[
+            pltpu.SemaphoreType.DMA((rows * cores,)),
+            pltpu.SemaphoreType.DMA((rows * cores,)),
+            pltpu.SemaphoreType.DMA,
+        ],
+        compiler_params=pltpu.CompilerParams(collective_id=identity, has_side_effects=True),
+    )(blocks)
+
+
 def local(images, rate_vectors, epoch_times):
     loc_epochs, loc_rows, length = images.shape
     row_count = lax.axis_size("row")
@@ -82,7 +135,7 @@
     spectrum = jnp.einsum("erc,cl->erl", images, rowwise, preferred_element_type=jnp.float32)
     spectrum = spectrum.astype(jnp.bfloat16).reshape(loc_epochs, loc_rows, devices, lanes)
     sent = spectrum.transpose(2, 0, 1, 3)
-    got = lax.all_to_all(sent, ("row", "epoch"), split_axis=0, concat_axis=0, tiled=True)
+    got = exchange(sent, row_count, epoch_count, 0)
     got = got.reshape(row_count, epoch_count * loc_epochs, loc_rows, lanes)
     pairs = jnp.einsum(
         "uir,ierl->eul",
@@ -108,7 +161,7 @@
     back = back.astype(jnp.bfloat16)
     back = back.reshape(epoch_count, rates // epoch_count, row_count, loc_rows, lanes)
     back = back.transpose(2, 0, 1, 3, 4).reshape(devices, rates // epoch_count, loc_rows, lanes)
-    returned = lax.all_to_all(back, ("row", "epoch"), split_axis=0, concat_axis=0, tiled=True)
+    returned = exchange(back, row_count, epoch_count, 1)
     return jnp.einsum("dkrl,dlc->krc", returned, inverse, preferred_element_type=jnp.float32)
 
 

time: 126 us -> 124 us (0.984)
  Pallas kernels: 0 us -> 78 us
  waiting for transfers between devices: 46.3 us -> 0 us
  blocking collectives: 29.5 us -> 0 us
  starting transfers between devices: 6.55 us -> 0 us
  matrix products: 29.3 us -> 31.2 us
  other arithmetic: 4.05 us -> 5.38 us
    pallas_call x0 -> x2, Pallas kernels: none -> 78 us  [exchange(): pl.pallas_call(functools.partial(exchange_kernel, rows, cores), out_shape...]
    all_to_all x1 -> x0, waiting for transfers between devices: 46.3 us -> none  [local(): lax.all_to_all(sent, ('row', 'epoch'), split_axis=0, concat_axis=0, tiled...]
    all_to_all x1 -> x0, blocking collectives: 29.5 us -> none  [local(): lax.all_to_all(back, ('row', 'epoch'), split_axis=0, concat_axis=0, tiled...]
    all_to_all x1 -> x0, starting transfers between devices: 6.55 us -> none  [local(): lax.all_to_all(sent, ('row', 'epoch'), split_axis=0, concat_axis=0, tiled...]
    reshape x0 -> x1, local copies, waits for them, and re-layouts: none -> 1.71 us  [local(): back.reshape(epoch_count, rates // epoch_count, row_count, loc_rows, lanes)]
    unnamed x9 -> x5, local copies, waits for them, and re-layouts: 1.9 us -> 0.31 us
  transfers between devices with their start and end apart: 1 -> 0, of which waited for: 1 -> 0; matrix products, arithmetic and copies ran while one was open for 1% -> 0% of each run, Pallas kernels for 0% -> 0%
where the time goes in v3:
time: 124 us; the launch traced here: 123 us
  Pallas kernels  78 us (63%)
  matrix products  31.2 us (25%)
  local copies, waits for them, and re-layouts  8.77 us (7%)
  other arithmetic  5.38 us (4%)
    pallas_call x2, Pallas kernels, exchange(): pl.pallas_call(functools.partial(exchange_kernel, rows, cores), out_shape...  78 us
    dot_general x1, matrix products, local(): jnp.einsum('erc,cl->erl', images, rowwise, preferred_element_type=jnp.flo...  9.17 us
    dot_general x1, matrix products, local(): jnp.einsum('uir,ierl->eul', forward.reshape(length, row_count, loc_rows),...  8.77 us
    dot_general x1, matrix products, local(): jnp.einsum('dkrl,dlc->krc', returned, inverse, preferred_element_type=jnp...  7.5 us
    dot_general x1, matrix products, local(): jnp.einsum('ur,kul->krl', forward, stacked, preferred_element_type=jnp.fl...  5.75 us
    reshape x1, local copies, waits for them, and re-layouts, local(): spectrum.astype(jnp.bfloat16).reshape(loc_epochs, loc_rows, devices, lanes)  3.94 us

profile of v3, /device:TPU:11, one launch (start us, length us, event | category | flops | bytes accessed | tf_op | source)
XLA Modules:
  0.0 123.4 jit_solution(14376115781877565119)
XLA Ops:
  0.0 0.0 copy-start
  0.0 1.1 slice_reduce_fusion.1
  1.1 0.7 and_select_fusion.4
  1.8 0.8 fusion.19
  2.6 0.1 select_multiply_fusion.5
  2.8 0.1 pad_maximum_fusion.2
  2.9 0.1 pad_maximum_fusion.4
  2.9 0.4 multiply_select_fusion.2
  3.3 0.0 copy-done
  3.3 9.2 %convolution_convert_fusion = bf16[2048,2,256]{2,0,1:T(8,128)(2,1)} fusion(bf16[2048,2048,1]{0,1,2:T(8,128)(2,1)} %constant.102, bf16[2,256,2048]{2,1,0:T(8,128)(2,1)S(1)} %copy-done), kind=kOutput, calls=%fused_computation.9 | convolution fusion | flops 4296015872 | bytes 12582912 | tf_op jit(solution)/shard_map/erc,cl->erl/dot_general | solution.py:135
  12.5 3.9 %copy.16 = bf16[2,256,16,128]{3,1,0,2:T(8,128)(2,1)} copy(bf16[2,256,16,128]{1,3,2,0:T(8,128)(2,1)} %bitcast.43) | data formatting | bytes 4194304 | tf_op jit(solution)/shard_map/reshape | solution.py:136
  16.4 50.6 %shard_map.64 = bf16[16,2,256,128]{3,2,1,0:T(8,128)(2,1)} custom-call(bf16[16,2,256,128]{3,2,1,0:T(8,128)(2,1)} %bitcast.39), custom_call_target="tpu_custom_call" | custom-call | tf_op jit(solution)/shard_map/pallas_call | solution.py:106
  67.0 8.8 %convolution_bitcast_fusion = f32[4,2048,128]{1,2,0:T(8,128)S(1)} fusion(bf16[2048,8,256,1]{2,0,3,1:T(8,128)(2,1)} %constant.103, bf16[8,4,256,128]{3,2,1,0:T(8,128)(2,1)} %bitcast.42), kind=kOutput, calls=%fused_computation.8 | convolution fusion | flops 4294967296 | bytes 14680064 | tf_op jit(solution)/shard_map/uir,ierl->eul/dot_general | solution.py:140
  75.8 0.3 fusion.37
  76.1 1.2 multiply_subtract_fusion
  77.3 1.4 %fusion.35 = (f32[2,4,1024,64]{2,3,1,0:T(8,128)S(1)}, f32[2,4,1024,64]{2,3,1,0:T(8,128)S(1)}, f32[2,4,1024,64]{2,3,1,0:T(8,128)S(1)}, f32[2,4,1024,64]{2,3,1,0:T(8,128)S(1)}) fusion(f32[2,4,1024,128]{2,3,1,0:T(8,128)S(1)} %get-tuple-element.11, f32[2,4,1024,128]{2,3,1,0:T(8,128)S(1)} %get-tuple-element.12), kind=kLoop, calls=%fused_computation.89 | loop fusion | bytes 16777216 | tf_op jit(solution)/shard_map/slice | solution.py:150
  78.8 2.0 %fusion.1 = (bf16[2,1024,128]{1,2,0:T(8,128)(2,1)S(1)}, bf16[2,1024,128]{1,2,0:T(8,128)(2,1)S(1)}) fusion(f32[2,4,1024,64]{2,3,1,0:T(8,128)S(1)} %get-tuple-element.40, f32[2,4,1024,64]{2,3,1,0:T(8,128)S(1)} %get-tuple-element.41, f32[2,4,1024,128]{2,3,1,0:T(8,128)S(1)} %get-tuple-element.12, f32[2,4,128]{2,1,0:T(4,128)S(1)} %get-tuple-element.45, ...), kind=kLoop, calls=%fused_computation.2 | loop fusion | flops 12058624 | bytes 17843200 | tf_op jit(solution)/shard_map/reduce_sum | solution.py:157
  80.8 5.8 %convolution_convert_fusion.1 = bf16[2,128,2048]{2,1,0:T(8,128)(2,1)S(1)} fusion(bf16[2048,2048,1]{1,0,2:T(8,128)(2,1)} %constant.104, bf16[2,1024,128]{1,2,0:T(8,128)(2,1)S(1)} %get-tuple-element.6, bf16[2,1024,128]{1,2,0:T(8,128)(2,1)S(1)} %get-tuple-element.5), kind=kOutput, calls=%fused_computation.11 | convolution fusion | flops 2150105088 | bytes 10485760 | tf_op jit(solution)/shard_map/ur,kul->krl/dot_general | solution.py:160
  86.6 0.3 copy.27
  86.9 1.7 %copy.22 = bf16[2,1,8,256,128]{4,3,0,2,1:T(8,128)(2,1)} copy(bf16[2,1,8,256,128]{3,2,4,0,1:T(8,128)(2,1)S(1)} %bitcast.40) | data formatting | bytes 2097152 | tf_op jit(solution)/shard_map/reshape | solution.py:162
  88.6 27.3 %shard_map.65 = bf16[16,1,256,128]{3,2,1,0:T(8,128)(2,1)} custom-call(bf16[16,1,256,128]{3,2,1,0:T(8,128)(2,1)} %bitcast.41), custom_call_target="tpu_custom_call" | custom-call | tf_op jit(solution)/shard_map/pallas_call | solution.py:106
  115.9 0.0 copy-start.1
  115.9 7.5 %convolution_bitcast_fusion.1 = f32[1,256,2048]{2,1,0:T(8,128)} fusion(bf16[16,128,2048]{2,1,0:T(8,128)(2,1)} %constant.101, bf16[16,1,256,128]{3,2,1,0:T(8,128)(2,1)} %shard_map.65), kind=kOutput, calls=%fused_computation.10 | convolution fusion | flops 2147483648 | bytes 11534336 | tf_op jit(solution)/shard_map/dkrl,dlc->krc/dot_general | solution.py:165
  123.4 0.0 copy-done.1
  (4 shorter events, 0.0 us)
Async XLA Ops:
  0.0 3.3 %copy-start = (bf16[2,256,2048]{2,1,0:T(8,128)(2,1)S(1)}, bf16[2,256,2048]{2,1,0:T(8,128)(2,1)}, u32[]{:S(2)}) copy-start(bf16[2,256,2048]{2,1,0:T(8,128)(2,1)} %param.6) | copy-start | bytes 6291460
  115.9 7.5 %copy-start.1 = (bf16[2,256,2048]{2,1,0:T(8,128)(2,1)S(1)}, bf16[2,256,2048]{2,1,0:T(8,128)(2,1)}, u32[]{:S(2)}) copy-start(bf16[2,256,2048]{2,1,0:T(8,128)(2,1)} %param.6) | copy-start | bytes 6291460

commit v4 on v1

--- a/solution.py
+++ b/solution.py
@@ -6,6 +6,8 @@
 import ml_dtypes
 import numpy as np
 from jax import lax
+from jax.experimental import pallas as pl
+from jax.experimental.pallas import tpu as pltpu
 from jax.sharding import PartitionSpec as P
 
 SUBPIX = 16
@@ -64,6 +66,90 @@
     return row_cos, row_sin, same, swap, first_same, first_swap
 
 
+def send_kernel(rows, cores, table_left, fixed, table, dst, stage, send_sem, recv_sem, own_sem):
+    count = rows * cores
+    lanes = stage.shape[2]
+    row, core = lax.axis_index("row"), lax.axis_index("epoch")
+    me = row * cores + core
+    barrier = pltpu.get_barrier_semaphore()
+
+    def place(device):
+        return {"row": lax.div(device, cores), "epoch": lax.rem(device, cores)}
+
+    for step in range(1, count):
+        pl.semaphore_signal(
+            barrier,
+            inc=1,
+            device_id=place(lax.rem(me + step, count)),
+            device_id_type=pl.DeviceIdType.MESH,
+        )
+    pl.semaphore_wait(barrier, count - 1)
+
+    def remote(device, slot):
+        return pltpu.make_async_remote_copy(
+            src_ref=stage.at[device],
+            dst_ref=dst.at[slot],
+            send_sem=send_sem.at[device],
+            recv_sem=recv_sem.at[slot],
+            device_id=place(device),
+            device_id_type=pl.DeviceIdType.MESH,
+        )
+
+    def multiply(chip):
+        left, right = (table[chip], fixed[...]) if table_left else (fixed[...], table[chip])
+        block = jnp.dot(left, right, preferred_element_type=jnp.float32).astype(stage.dtype)
+        for other in range(cores):
+            stage[chip * cores + other] = block[:, other * lanes : (other + 1) * lanes]
+
+    def one_chip(step, carry):
+        offset = rows // 2 + ((step + 1) // 2) * (2 * (step % 2) - 1)
+        chip = lax.rem(row + offset, rows)
+        multiply(chip)
+        for other in range(cores):
+            remote(chip * cores + other, me).start()
+        return carry
+
+    lax.fori_loop(0, rows - 1, one_chip, 0)
+    multiply(row)
+    for step in range(1, cores):
+        remote(row * cores + lax.rem(core + step, cores), me).start()
+    own = pltpu.make_async_copy(stage.at[me], dst.at[me], own_sem)
+    own.start()
+    own.wait()
+
+    def finish(step, carry):
+        device = lax.rem(me + step, count)
+        remote(device, device).wait()
+        return carry
+
+    lax.fori_loop(1, count, finish, 0)
+
+
+def multiply_and_send(fixed, table, rows, cores, table_left, identity):
+    height = table.shape[1] if table_left else fixed.shape[0]
+    width = (fixed.shape[1] if table_left else table.shape[2]) // cores
+    shape = (rows * cores, height, width)
+    return pl.pallas_call(
+        functools.partial(send_kernel, rows, cores, table_left),
+        out_shape=jax.ShapeDtypeStruct(shape, jnp.bfloat16),
+        in_specs=[pl.BlockSpec(memory_space=pltpu.VMEM)] * 2,
+        out_specs=pl.BlockSpec(memory_space=pl.ANY),
+        scratch_shapes=[
+            pltpu.VMEM(shape, jnp.bfloat16),
+            pltpu.SemaphoreType.DMA((rows * cores,)),
+            pltpu.SemaphoreType.DMA((rows * cores,)),
+            pltpu.SemaphoreType.DMA,
+        ],
+        compiler_params=pltpu.CompilerParams(
+            collective_id=identity, has_side_effects=True, vmem_limit_bytes=40 * 2**20
+        ),
+    )(fixed, table)
+
+
+def exchange(blocks):
+    return lax.all_to_all(blocks, ("row", "epoch"), split_axis=0, concat_axis=0, tiled=True)
+
+
 def local(images, rate_vectors, epoch_times):
     loc_epochs, loc_rows, length = images.shape
     row_count = lax.axis_size("row")
@@ -79,10 +165,16 @@
     rowwise = jnp.asarray(np.ascontiguousarray(lane_table.T))
     inverse = jnp.asarray(lane_table).reshape(devices, lanes, length)
     forward = jnp.asarray(table)
-    spectrum = jnp.einsum("erc,cl->erl", images, rowwise, preferred_element_type=jnp.float32)
-    spectrum = spectrum.astype(jnp.bfloat16).reshape(loc_epochs, loc_rows, devices, lanes)
-    sent = spectrum.transpose(2, 0, 1, 3)
-    got = lax.all_to_all(sent, ("row", "epoch"), split_axis=0, concat_axis=0, tiled=True)
+    fused = lanes % 128 == 0 and loc_rows % 16 == 0 and rates == epoch_count and row_count % 2 == 0
+    if fused:
+        chips = lane_table.T.reshape(length, row_count, epoch_count * lanes).transpose(1, 0, 2)
+        chips = jnp.asarray(np.ascontiguousarray(chips))
+        flat = images.reshape(loc_epochs * loc_rows, length)
+        got = multiply_and_send(flat, chips, row_count, epoch_count, False, 0)
+    else:
+        spectrum = jnp.einsum("erc,cl->erl", images, rowwise, preferred_element_type=jnp.float32)
+        spectrum = spectrum.astype(jnp.bfloat16).reshape(loc_epochs, loc_rows, devices, lanes)
+        got = exchange(spectrum.transpose(2, 0, 1, 3))
     got = got.reshape(row_count, epoch_count * loc_epochs, loc_rows, lanes)
     pairs = jnp.einsum(
         "uir,ierl->eul",
@@ -104,11 +196,18 @@
     sum_even = jnp.sum(same_even * moved_even + swap_even * swapped(moved_even), axis=1)
     sum_odd = jnp.sum(same[:, :, None] * moved_odd + swap[:, :, None] * swapped(moved_odd), axis=1)
     stacked = jnp.concatenate([sum_even, sum_odd], axis=1).astype(jnp.bfloat16)
-    back = jnp.einsum("ur,kul->krl", forward, stacked, preferred_element_type=jnp.float32)
-    back = back.astype(jnp.bfloat16)
-    back = back.reshape(epoch_count, rates // epoch_count, row_count, loc_rows, lanes)
-    back = back.transpose(2, 0, 1, 3, 4).reshape(devices, rates // epoch_count, loc_rows, lanes)
-    returned = lax.all_to_all(back, ("row", "epoch"), split_axis=0, concat_axis=0, tiled=True)
+    if fused:
+        chips = table.T.reshape(row_count, loc_rows, length)
+        chips = jnp.asarray(np.ascontiguousarray(chips))
+        flat = stacked.transpose(1, 0, 2).reshape(length, rates * lanes)
+        returned = multiply_and_send(flat, chips, row_count, epoch_count, True, 1)
+        returned = returned[:, None]
+    else:
+        back = jnp.einsum("ur,kul->krl", forward, stacked, preferred_element_type=jnp.float32)
+        back = back.astype(jnp.bfloat16)
+        back = back.reshape(epoch_count, rates // epoch_count, row_count, loc_rows, lanes)
+        back = back.transpose(2, 0, 1, 3, 4)
+        returned = exchange(back.reshape(devices, rates // epoch_count, loc_rows, lanes))
     return jnp.einsum("dkrl,dlc->krc", returned, inverse, preferred_element_type=jnp.float32)
 
 

time: 126 us -> 107 us (0.85)
  Pallas kernels: 0 us -> 77.8 us
  waiting for transfers between devices: 46.3 us -> 0 us
  blocking collectives: 29.5 us -> 0 us
  matrix products: 29.3 us -> 10.6 us
  starting transfers between devices: 6.55 us -> 0 us
  local copies, waits for them, and re-layouts: 8.78 us -> 12.1 us
  other arithmetic: 4.05 us -> 5.73 us
    pallas_call x0 -> x2, Pallas kernels: none -> 77.8 us  [multiply_and_send(): pl.pallas_call(functools.partial(send_kernel, rows, cores, table_left), o...]
    all_to_all x1 -> x0, waiting for transfers between devices: 46.3 us -> none  [local(): lax.all_to_all(sent, ('row', 'epoch'), split_axis=0, concat_axis=0, tiled...]
    all_to_all x1 -> x0, blocking collectives: 29.5 us -> none  [local(): lax.all_to_all(back, ('row', 'epoch'), split_axis=0, concat_axis=0, tiled...]
    dot_general x2 -> x0, matrix products: 14.9 us -> none  [the longest x1 9.15 us: local(): jnp.einsum('erc,cl->erl', images, rowwise, preferred_element_type=jnp.flo...]
    unnamed x9 -> x10, local copies, waits for them, and re-layouts: 1.9 us -> 8.89 us
    all_to_all x1 -> x0, starting transfers between devices: 6.55 us -> none  [local(): lax.all_to_all(sent, ('row', 'epoch'), split_axis=0, concat_axis=0, tiled...]
    reshape x1 -> x0, local copies, waits for them, and re-layouts: 3.95 us -> none  [local(): spectrum.astype(jnp.bfloat16).reshape(loc_epochs, loc_rows, devices, lanes)]
    dot_general x1, matrix products: 8.07 us -> 4.55 us  [local(): jnp.einsum('uir,ierl->eul', forward.reshape(length, row_count, loc_rows),...]
  transfers between devices with their start and end apart: 1 -> 0, of which waited for: 1 -> 0; matrix products, arithmetic and copies ran while one was open for 1% -> 0% of each run, Pallas kernels for 0% -> 0%
where the time goes in v4:
time: 107 us; the launch traced here: 106 us
  Pallas kernels  77.8 us (73%)
  local copies, waits for them, and re-layouts  12.1 us (11%)
  matrix products  10.6 us (10%)
  other arithmetic  5.73 us (5%)
    pallas_call x2, Pallas kernels, multiply_and_send(): pl.pallas_call(functools.partial(send_kernel, rows, cores, table_left), o...  77.8 us
    unnamed x10, local copies, waits for them, and re-layouts  8.89 us
    dot_general x1, matrix products, local(): jnp.einsum('dkrl,dlc->krc', returned, inverse, preferred_element_type=jnp...  6.06 us
    dot_general x1, matrix products, local(): jnp.einsum('uir,ierl->eul', forward.reshape(length, row_count, loc_rows),...  4.55 us

profile of v4, /device:TPU:11, one launch (start us, length us, event | category | flops | bytes accessed | tf_op | source)
XLA Modules:
  0.0 106.4 jit_solution(6283166427046301403)
XLA Ops:
  0.0 1.0 slice_reduce_fusion.1
  1.0 0.7 and_select_fusion.4
  1.7 0.8 fusion.16
  2.5 0.1 select_multiply_fusion.5
  2.7 0.1 pad_maximum_fusion
  2.8 0.1 pad_maximum_fusion.2
  2.8 0.4 multiply_select_fusion.2
  3.2 0.0 copy-start.1
  3.2 3.4 %copy-done.1 = bf16[8,2048,256]{2,1,0:T(8,128)(2,1)S(1)} copy-done((bf16[8,2048,256]{2,1,0:T(8,128)(2,1)S(1)}, bf16[8,2048,256]{2,1,0:T(8,128)(2,1)}, u32[]{:S(2)}) %copy-start.1) | copy-done | bytes 8388632
  6.6 1.6 %copy-done.2 = bf16[2,256,2048]{2,1,0:T(8,128)(2,1)S(1)} copy-done((bf16[2,256,2048]{2,1,0:T(8,128)(2,1)S(1)}, bf16[2,256,2048]{2,1,0:T(8,128)(2,1)}, u32[]{:S(2)}) %copy-start.2) | copy-done | bytes 2097176
  8.2 51.1 %shard_map.73 = bf16[16,512,128]{2,1,0:T(8,128)(2,1)S(1)} custom-call(bf16[512,2048]{1,0:T(8,128)(2,1)S(1)} %bitcast.22, bf16[8,2048,256]{2,1,0:T(8,128)(2,1)S(1)} %copy-done.1), custom_call_target="tpu_custom_call" | custom-call | tf_op jit(solution)/shard_map/pallas_call | solution.py:132
  59.3 0.0 copy-done.3
  59.3 4.6 %convolution_bitcast_fusion = f32[4,2048,128]{1,2,0:T(8,128)S(1)} fusion(bf16[8,4,256,128]{3,2,1,0:T(8,128)(2,1)S(1)} %bitcast.23, bf16[2048,8,256,1]{2,0,3,1:T(8,128)(2,1)S(1)} %copy-done.3), kind=kOutput, calls=%fused_computation.8 | convolution fusion | flops 4294967296 | bytes 14680064 | tf_op jit(solution)/shard_map/uir,ierl->eul/dot_general | solution.py:179
  63.9 0.6 fusion.33
  64.5 1.6 %multiply_subtract_fusion = (f32[2,4,1024,128]{2,3,1,0:T(8,128)S(1)}, f32[2,4,1024,128]{2,3,1,0:T(8,128)S(1)}) fusion(f32[4,1024,128]{1,2,0:T(8,128)S(1)} %get-tuple-element.18, f32[2,4,1024]{2,1,0:T(4,128)S(1)} %get-tuple-element.20, f32[4,1024,128]{1,2,0:T(8,128)S(1)} %get-tuple-element.17, f32[2,4,1024]{2,1,0:T(4,128)S(1)} %get-tuple-element.19), kind=kLoop, calls=%fused_computation.6 | loop fusion | flops 6291456 | bytes 12648448 | tf_op jit(solution)/shard_map/sub | solution.py:192
  66.0 1.7 %fusion.31 = (f32[2,4,1024,64]{2,3,1,0:T(8,128)S(1)}, f32[2,4,1024,64]{2,3,1,0:T(8,128)S(1)}, f32[2,4,1024,64]{2,3,1,0:T(8,128)S(1)}, f32[2,4,1024,64]{2,3,1,0:T(8,128)S(1)}) fusion(f32[2,4,1024,128]{2,3,1,0:T(8,128)S(1)} %get-tuple-element.11, f32[2,4,1024,128]{2,3,1,0:T(8,128)S(1)} %get-tuple-element.12), kind=kLoop, calls=%fused_computation.84 | loop fusion | bytes 16777216 | tf_op jit(solution)/shard_map/slice | solution.py:189
  67.7 1.9 %fusion.1 = (bf16[2,1024,128]{1,2,0:T(8,128)(2,1)S(1)}, bf16[2,1024,128]{1,2,0:T(8,128)(2,1)S(1)}) fusion(f32[2,4,1024,64]{2,3,1,0:T(8,128)S(1)} %get-tuple-element.40, f32[2,4,1024,64]{2,3,1,0:T(8,128)S(1)} %get-tuple-element.41, f32[2,4,1024,128]{2,3,1,0:T(8,128)S(1)} %get-tuple-element.12, f32[2,4,128]{2,1,0:T(4,128)S(1)} %get-tuple-element.45, ...), kind=kLoop, calls=%fused_computation.2 | loop fusion | flops 12058624 | bytes 17843200 | tf_op jit(solution)/shard_map/reduce_sum | solution.py:196
  69.6 0.3 copy.17
  69.8 0.3 copy.18
  70.1 0.1 copy_bitcast_fusion.fixed
  70.2 0.0 copy-start
  70.3 3.4 %copy-done = bf16[8,256,2048]{2,1,0:T(8,128)(2,1)S(1)} copy-done((bf16[8,256,2048]{2,1,0:T(8,128)(2,1)S(1)}, bf16[8,256,2048]{2,1,0:T(8,128)(2,1)}, u32[]{:S(2)}) %copy-start) | copy-done | bytes 8388632
  73.6 26.7 %shard_map.74 = bf16[16,256,128]{2,1,0:T(8,128)(2,1)S(1)} custom-call(bf16[2048,256]{1,0:T(8,128)(2,1)S(1)} %copy_bitcast_fusion.fixed, bf16[8,256,2048]{2,1,0:T(8,128)(2,1)S(1)} %copy-done), custom_call_target="tpu_custom_call" | custom-call | tf_op jit(solution)/shard_map/pallas_call | solution.py:132
  100.3 6.1 %convolution_bitcast_fusion.1 = f32[1,256,2048]{2,1,0:T(8,128)} fusion(bf16[16,256,128]{2,1,0:T(8,128)(2,1)S(1)} %shard_map.74, bf16[16,128,2048]{2,1,0:T(8,128)(2,1)} %constant.104), kind=kOutput, calls=%fused_computation.9 | convolution fusion | flops 2147483648 | bytes 11534336 | tf_op jit(solution)/shard_map/dkrl,dlc->krc/dot_general | solution.py:211
  (6 shorter events, 0.0 us)
Async XLA Ops:
  3.2 3.4 %copy-start.1 = (bf16[8,2048,256]{2,1,0:T(8,128)(2,1)S(1)}, bf16[8,2048,256]{2,1,0:T(8,128)(2,1)}, u32[]{:S(2)}) copy-start(bf16[8,2048,256]{2,1,0:T(8,128)(2,1)} %constant.100.clone.table) | copy-start | bytes 25165828
  6.6 1.6 %copy-start.2 = (bf16[2,256,2048]{2,1,0:T(8,128)(2,1)S(1)}, bf16[2,256,2048]{2,1,0:T(8,128)(2,1)}, u32[]{:S(2)}) copy-start(bf16[2,256,2048]{2,1,0:T(8,128)(2,1)} %param.7) | copy-start | bytes 6291460
  8.2 51.2 %copy-start.3 = (bf16[2048,8,256,1]{2,0,3,1:T(8,128)(2,1)S(1)}, bf16[2048,8,256,1]{2,0,3,1:T(8,128)(2,1)}, u32[]{:S(2)}) copy-start(bf16[2048,8,256,1]{2,0,3,1:T(8,128)(2,1)} %constant.105) | copy-start | bytes 25165828
  70.2 3.4 %copy-start = (bf16[8,256,2048]{2,1,0:T(8,128)(2,1)S(1)}, bf16[8,256,2048]{2,1,0:T(8,128)(2,1)}, u32[]{:S(2)}) copy-start(bf16[8,256,2048]{2,1,0:T(8,128)(2,1)} %constant.101.clone.table) | copy-start | bytes 25165828

commit v5 on v4

--- a/solution.py
+++ b/solution.py
@@ -66,11 +66,26 @@
     return row_cos, row_sin, same, swap, first_same, first_swap
 
 
-def send_kernel(rows, cores, table_left, fixed, table, dst, stage, send_sem, recv_sem, own_sem):
+def send_kernel(
+    rows, cores, table_left, fixed, source, dst, stage, table, load_sem, send_sem, recv_sem, own_sem
+):
     count = rows * cores
     lanes = stage.shape[2]
     row, core = lax.axis_index("row"), lax.axis_index("epoch")
     me = row * cores + core
+
+    def chip_at(step):
+        offset = rows // 2 + ((step + 1) // 2) * (2 * (step % 2) - 1)
+        return lax.rem(row + offset, rows)
+
+    def load(chip):
+        return pltpu.make_async_copy(source.at[chip], table.at[chip], load_sem.at[chip])
+
+    def start_load(step, carry):
+        load(chip_at(step)).start()
+        return carry
+
+    lax.fori_loop(0, rows, start_load, 0)
     barrier = pltpu.get_barrier_semaphore()
 
     def place(device):
@@ -96,14 +111,14 @@
         )
 
     def multiply(chip):
+        load(chip).wait()
         left, right = (table[chip], fixed[...]) if table_left else (fixed[...], table[chip])
         block = jnp.dot(left, right, preferred_element_type=jnp.float32).astype(stage.dtype)
         for other in range(cores):
             stage[chip * cores + other] = block[:, other * lanes : (other + 1) * lanes]
 
     def one_chip(step, carry):
-        offset = rows // 2 + ((step + 1) // 2) * (2 * (step % 2) - 1)
-        chip = lax.rem(row + offset, rows)
+        chip = chip_at(step)
         multiply(chip)
         for other in range(cores):
             remote(chip * cores + other, me).start()
@@ -132,16 +147,21 @@
     return pl.pallas_call(
         functools.partial(send_kernel, rows, cores, table_left),
         out_shape=jax.ShapeDtypeStruct(shape, jnp.bfloat16),
-        in_specs=[pl.BlockSpec(memory_space=pltpu.VMEM)] * 2,
+        in_specs=[
+            pl.BlockSpec(memory_space=pltpu.VMEM),
+            pl.BlockSpec(memory_space=pl.ANY),
+        ],
         out_specs=pl.BlockSpec(memory_space=pl.ANY),
         scratch_shapes=[
             pltpu.VMEM(shape, jnp.bfloat16),
+            pltpu.VMEM(table.shape, jnp.bfloat16),
+            pltpu.SemaphoreType.DMA((rows,)),
             pltpu.SemaphoreType.DMA((rows * cores,)),
             pltpu.SemaphoreType.DMA((rows * cores,)),
             pltpu.SemaphoreType.DMA,
         ],
         compiler_params=pltpu.CompilerParams(
-            collective_id=identity, has_side_effects=True, vmem_limit_bytes=40 * 2**20
+            collective_id=identity, has_side_effects=True, vmem_limit_bytes=56 * 2**20
         ),
     )(fixed, table)
 

time: 107 us -> 106 us (level)
  local copies, waits for them, and re-layouts: 12.1 us -> 3.32 us
  matrix products: 10.6 us -> 15.1 us
  Pallas kernels: 77.8 us -> 81 us
    unnamed x10 -> x2, local copies, waits for them, and re-layouts: 8.89 us -> 0.54 us
    pallas_call x2, Pallas kernels: 77.8 us -> 81 us  [multiply_and_send(): pl.pallas_call(functools.partial(send_kernel, rows, cores, table_left), o...]
    dot_general x1, matrix products: 4.55 us -> 7.69 us  [local(): jnp.einsum('uir,ierl->eul', forward.reshape(length, row_count, loc_rows),...]
    dot_general x1, matrix products: 6.06 us -> 7.37 us  [local(): jnp.einsum('dkrl,dlc->krc', returned, inverse, preferred_element_type=jnp...]
where the time goes in v5:
time: 106 us
  Pallas kernels  81 us (76%)
  matrix products  15.1 us (14%)
  other arithmetic  6.48 us (6%)
  local copies, waits for them, and re-layouts  3.32 us (3%)
    pallas_call x2, Pallas kernels, multiply_and_send(): pl.pallas_call(functools.partial(send_kernel, rows, cores, table_left), o...  81 us
    dot_general x1, matrix products, local(): jnp.einsum('uir,ierl->eul', forward.reshape(length, row_count, loc_rows),...  7.69 us
    dot_general x1, matrix products, local(): jnp.einsum('dkrl,dlc->krc', returned, inverse, preferred_element_type=jnp...  7.37 us

profile of v5, /device:TPU:11, one launch (start us, length us, event | category | flops | bytes accessed | tf_op | source)
XLA Modules:
  0.0 106.0 jit_solution(5641580375911376071)
XLA Ops:
  0.0 1.0 slice_reduce_fusion.1
  1.0 0.7 and_select_fusion.4
  1.7 0.8 fusion.16
  2.5 0.1 select_multiply_fusion.5
  2.7 0.1 pad_maximum_fusion
  2.8 0.1 pad_maximum_fusion.2
  2.8 0.4 multiply_select_fusion.2
  3.2 52.9 %shard_map.73 = bf16[16,512,128]{2,1,0:T(8,128)(2,1)} custom-call(bf16[512,2048]{1,0:T(8,128)(2,1)} %bitcast.22, bf16[8,2048,256]{2,1,0:T(8,128)(2,1)} %constant.100.clone.source), custom_call_target="tpu_custom_call" | custom-call | tf_op jit(solution)/shard_map/pallas_call | solution.py:147
  56.1 7.7 %convolution_bitcast_fusion = f32[4,2048,128]{1,2,0:T(8,128)S(1)} fusion(bf16[8,4,256,128]{3,2,1,0:T(8,128)(2,1)} %bitcast.23, bf16[2048,8,256,1]{2,0,3,1:T(8,128)(2,1)} %constant.105), kind=kOutput, calls=%fused_computation.8 | convolution fusion | flops 4294967296 | bytes 14680064 | tf_op jit(solution)/shard_map/uir,ierl->eul/dot_general | solution.py:199
  63.8 0.6 fusion.33
  64.4 1.2 %multiply_subtract_fusion = (f32[2,4,1024,128]{2,3,1,0:T(8,128)S(1)}, f32[2,4,1024,128]{2,3,1,0:T(8,128)S(1)}) fusion(f32[4,1024,128]{1,2,0:T(8,128)S(1)} %get-tuple-element.18, f32[2,4,1024]{2,1,0:T(4,128)S(1)} %get-tuple-element.20, f32[4,1024,128]{1,2,0:T(8,128)S(1)} %get-tuple-element.17, f32[2,4,1024]{2,1,0:T(4,128)S(1)} %get-tuple-element.19), kind=kLoop, calls=%fused_computation.6 | loop fusion | flops 6291456 | bytes 12648448 | tf_op jit(solution)/shard_map/sub | solution.py:212
  65.6 1.2 %fusion.31 = (f32[2,4,1024,64]{2,3,1,0:T(8,128)S(1)}, f32[2,4,1024,64]{2,3,1,0:T(8,128)S(1)}, f32[2,4,1024,64]{2,3,1,0:T(8,128)S(1)}, f32[2,4,1024,64]{2,3,1,0:T(8,128)S(1)}) fusion(f32[2,4,1024,128]{2,3,1,0:T(8,128)S(1)} %get-tuple-element.11, f32[2,4,1024,128]{2,3,1,0:T(8,128)S(1)} %get-tuple-element.12), kind=kLoop, calls=%fused_computation.84 | loop fusion | bytes 16777216 | tf_op jit(solution)/shard_map/slice | solution.py:209
  66.9 2.0 %fusion.1 = (bf16[2,1024,128]{1,2,0:T(8,128)(2,1)S(1)}, bf16[2,1024,128]{1,2,0:T(8,128)(2,1)S(1)}) fusion(f32[2,4,1024,64]{2,3,1,0:T(8,128)S(1)} %get-tuple-element.40, f32[2,4,1024,64]{2,3,1,0:T(8,128)S(1)} %get-tuple-element.41, f32[2,4,1024,128]{2,3,1,0:T(8,128)S(1)} %get-tuple-element.12, f32[2,4,128]{2,1,0:T(4,128)S(1)} %get-tuple-element.45, ...), kind=kLoop, calls=%fused_computation.2 | loop fusion | flops 12058624 | bytes 17843200 | tf_op jit(solution)/shard_map/reduce_sum | solution.py:216
  68.9 0.3 copy.17
  69.1 0.3 copy.18
  69.4 1.1 %copy_bitcast_fusion.fixed = bf16[2048,256]{1,0:T(8,128)(2,1)} fusion(bf16[2,1024,128]{2,1,0:T(8,128)(2,1)S(1)} %copy.18, bf16[2,1024,128]{2,1,0:T(8,128)(2,1)S(1)} %copy.17), kind=kLoop, calls=%fused_computation.10 | loop fusion | flops 2097152 | bytes 2097152 | tf_op jit(solution)/shard_map/reshape | solution.py:222
  70.5 28.1 %shard_map.74 = bf16[16,256,128]{2,1,0:T(8,128)(2,1)} custom-call(bf16[2048,256]{1,0:T(8,128)(2,1)} %copy_bitcast_fusion.fixed, bf16[8,256,2048]{2,1,0:T(8,128)(2,1)} %constant.101.clone.source), custom_call_target="tpu_custom_call" | custom-call | tf_op jit(solution)/shard_map/pallas_call | solution.py:147
  98.6 7.4 %convolution_bitcast_fusion.1 = f32[1,256,2048]{2,1,0:T(8,128)} fusion(bf16[16,256,128]{2,1,0:T(8,128)(2,1)} %shard_map.74, bf16[16,128,2048]{2,1,0:T(8,128)(2,1)} %constant.104), kind=kOutput, calls=%fused_computation.9 | convolution fusion | flops 2147483648 | bytes 11534336 | tf_op jit(solution)/shard_map/dkrl,dlc->krc/dot_general | solution.py:231
  (4 shorter events, 0.0 us)

commit v6 on v5

--- a/solution.py
+++ b/solution.py
@@ -161,7 +161,7 @@
             pltpu.SemaphoreType.DMA,
         ],
         compiler_params=pltpu.CompilerParams(
-            collective_id=identity, has_side_effects=True, vmem_limit_bytes=56 * 2**20
+            collective_id=identity, has_side_effects=True, vmem_limit_bytes=50 * 2**20
         ),
     )(fixed, table)
 

time: 106 us -> 99 us (0.934)
  matrix products: 15.1 us -> 10.6 us
  other arithmetic: 6.48 us -> 5.25 us
  Pallas kernels: 81 us -> 79.9 us
    dot_general x1, matrix products: 7.69 us -> 4.55 us  [local(): jnp.einsum('uir,ierl->eul', forward.reshape(length, row_count, loc_rows),...]
    dot_general x1, matrix products: 7.37 us -> 6.06 us  [local(): jnp.einsum('dkrl,dlc->krc', returned, inverse, preferred_element_type=jnp...]
    pallas_call x2, Pallas kernels: 81 us -> 79.9 us  [multiply_and_send(): pl.pallas_call(functools.partial(send_kernel, rows, cores, table_left), o...]
where the time goes in v6:
time: 99 us; the launch traced here: 98.8 us
  Pallas kernels  79.9 us (81%)
  matrix products  10.6 us (11%)
  other arithmetic  5.25 us (5%)
  local copies, waits for them, and re-layouts  2.97 us (3%)
    pallas_call x2, Pallas kernels, multiply_and_send(): pl.pallas_call(functools.partial(send_kernel, rows, cores, table_left), o...  79.9 us
    dot_general x1, matrix products, local(): jnp.einsum('dkrl,dlc->krc', returned, inverse, preferred_element_type=jnp...  6.06 us
    dot_general x1, matrix products, local(): jnp.einsum('uir,ierl->eul', forward.reshape(length, row_count, loc_rows),...  4.55 us
    reduce_sum x1, other arithmetic, local(): jnp.sum(same_even * moved_even + swap_even * swapped(moved_even), axis=1)  2.05 us

profile of v6, /device:TPU:11, one launch (start us, length us, event | category | flops | bytes accessed | tf_op | source)
XLA Modules:
  0.0 98.8 jit_solution(13089456633137272791)
XLA Ops:
  0.0 1.0 slice_reduce_fusion.1
  1.0 0.7 and_select_fusion.4
  1.7 0.8 fusion.16
  2.5 0.1 select_multiply_fusion.5
  2.7 0.1 pad_maximum_fusion
  2.8 0.1 pad_maximum_fusion.2
  2.8 0.4 multiply_select_fusion.2
  3.2 0.0 copy-start
  3.2 53.0 %shard_map.73 = bf16[16,512,128]{2,1,0:T(8,128)(2,1)S(1)} custom-call(bf16[512,2048]{1,0:T(8,128)(2,1)} %bitcast.23, bf16[8,2048,256]{2,1,0:T(8,128)(2,1)} %constant.100.clone.source), custom_call_target="tpu_custom_call" | custom-call | tf_op jit(solution)/shard_map/pallas_call | solution.py:147
  56.2 0.0 copy-done
  56.2 4.6 %convolution_bitcast_fusion = f32[4,2048,128]{1,2,0:T(8,128)S(1)} fusion(bf16[8,4,256,128]{3,2,1,0:T(8,128)(2,1)S(1)} %bitcast.22, bf16[2048,8,256,1]{2,0,3,1:T(8,128)(2,1)S(1)} %copy-done), kind=kOutput, calls=%fused_computation.8 | convolution fusion | flops 4294967296 | bytes 14680064 | tf_op jit(solution)/shard_map/uir,ierl->eul/dot_general | solution.py:199
  60.8 0.4 fusion.33
  61.2 0.9 multiply_subtract_fusion
  62.1 1.0 %fusion.31 = (f32[2,4,1024,64]{2,3,1,0:T(8,128)S(1)}, f32[2,4,1024,64]{2,3,1,0:T(8,128)S(1)}, f32[2,4,1024,64]{2,3,1,0:T(8,128)S(1)}, f32[2,4,1024,64]{2,3,1,0:T(8,128)S(1)}) fusion(f32[2,4,1024,128]{2,3,1,0:T(8,128)S(1)} %get-tuple-element.11, f32[2,4,1024,128]{2,3,1,0:T(8,128)S(1)} %get-tuple-element.12), kind=kLoop, calls=%fused_computation.84 | loop fusion | bytes 16777216 | tf_op jit(solution)/shard_map/slice | solution.py:209
  63.1 2.0 %fusion.1 = (bf16[2,1024,128]{1,2,0:T(8,128)(2,1)S(1)}, bf16[2,1024,128]{1,2,0:T(8,128)(2,1)S(1)}) fusion(f32[2,4,1024,64]{2,3,1,0:T(8,128)S(1)} %get-tuple-element.40, f32[2,4,1024,64]{2,3,1,0:T(8,128)S(1)} %get-tuple-element.41, f32[2,4,1024,128]{2,3,1,0:T(8,128)S(1)} %get-tuple-element.12, f32[2,4,128]{2,1,0:T(4,128)S(1)} %get-tuple-element.45, ...), kind=kLoop, calls=%fused_computation.2 | loop fusion | flops 12058624 | bytes 17843200 | tf_op jit(solution)/shard_map/reduce_sum | solution.py:216
  65.2 0.3 copy.17
  65.4 0.3 copy.18
  65.7 0.1 copy_bitcast_fusion.fixed
  65.9 26.9 %shard_map.74 = bf16[16,256,128]{2,1,0:T(8,128)(2,1)S(1)} custom-call(bf16[2048,256]{1,0:T(8,128)(2,1)S(1)} %copy_bitcast_fusion.fixed, bf16[8,256,2048]{2,1,0:T(8,128)(2,1)} %constant.101.clone.source), custom_call_target="tpu_custom_call" | custom-call | tf_op jit(solution)/shard_map/pallas_call | solution.py:147
  92.8 6.1 %convolution_bitcast_fusion.1 = f32[1,256,2048]{2,1,0:T(8,128)} fusion(bf16[16,256,128]{2,1,0:T(8,128)(2,1)S(1)} %shard_map.74, bf16[16,128,2048]{2,1,0:T(8,128)(2,1)} %constant.104), kind=kOutput, calls=%fused_computation.9 | convolution fusion | flops 2147483648 | bytes 11534336 | tf_op jit(solution)/shard_map/dkrl,dlc->krc/dot_general | solution.py:231
  (4 shorter events, 0.0 us)
Async XLA Ops:
  3.2 53.0 %copy-start = (bf16[2048,8,256,1]{2,0,3,1:T(8,128)(2,1)S(1)}, bf16[2048,8,256,1]{2,0,3,1:T(8,128)(2,1)}, u32[]{:S(2)}) copy-start(bf16[2048,8,256,1]{2,0,3,1:T(8,128)(2,1)} %constant.105) | copy-start | bytes 25165828
